TPU v7x, 256 devices: a whole 4x4x8 slice. The times are simulated.
256 devices in a mesh: dp: 16 (over x, y), head: 16 (over z, core).
Axes of the slice: x: 4, y: 4, z: 8, core: 2. Of those that a mesh axis runs over, the one named last changes fastest.
Arguments:
- student_patches: bfloat16 [16384, 256], P('dp'), may hold values from -100 to 100
- teacher_patches: bfloat16 [16384, 256], P('dp'), may hold values from -20 to 20
- mask_rows: int32 [8192], P('dp'), may hold values from 0 to 1023
- prototypes: bfloat16 [256, 131072], P(None, 'head'), may hold values from -3 to 3
Outputs:
- grad_patches: float32 [16384, 256], P('dp')
- grad_prototypes: float32 [256, 131072], P('dp', 'head')
- loss: float32 [], replicated
Inputs may be any that keep to these rules, and one draw needn't show every extreme that they name: Entry i names patch row (i // 512) * 1024 + mask_rows[i]; entries may repeat.
All inputs are finite; a program needn't handle non-finite values.
Results may differ from a plain program's by a relative error of at most 0.0045.
Values sent between devices are 32-bit elements; how exact they have to be, the bound alone decides.
A program may use at most 128 MiB of HBM per device.

v0:
```python
import jax
import jax.numpy as jnp
from jax import lax
from jax.sharding import PartitionSpec as P

ITERS = 3


eps = 1e-06
teacher_temp = 0.04
student_temp = 0.1
loss_scale = 4096.0
highest = lax.Precision.HIGHEST


def unit_rows(values):
    inverse = lax.rsqrt(jnp.sum(values * values, axis=1, keepdims=True) + eps)
    return (values * inverse, inverse)


def on_device(student_patches, teacher_patches, mask_rows, prototypes):
    row_count = mask_rows.shape[0]
    total_rows = row_count * lax.axis_size("dp")
    total_cols = prototypes.shape[1] * lax.axis_size("head")
    student_unit, inv_norm = unit_rows(
        jnp.take(student_patches, mask_rows, axis=0).astype(jnp.float32)
    )
    student_unit = student_unit.astype(jnp.bfloat16)
    teacher_unit = unit_rows(jnp.take(teacher_patches, mask_rows, axis=0).astype(jnp.float32))[
        0
    ].astype(jnp.bfloat16)
    weight = prototypes.astype(jnp.float32)
    col_inv = lax.rsqrt(jnp.sum(weight * weight, axis=0) + eps)
    normed = (weight * col_inv[None, :]).astype(jnp.bfloat16)
    teach_exp = jnp.exp(
        jnp.dot(teacher_unit, normed, preferred_element_type=jnp.float32) / teacher_temp
    )
    student_raw = jnp.dot(student_unit, normed, preferred_element_type=jnp.float32)
    exp_local = jnp.sum(jnp.exp(student_raw / student_temp), axis=1)
    sample_scale = jnp.ones((row_count,), jnp.float32)
    for sweep in range(ITERS):
        col_total = lax.psum(jnp.dot(sample_scale, teach_exp, precision=highest), "dp")
        col_scale = 1.0 / (total_cols * col_total)
        row_part = jnp.dot(teach_exp, col_scale, precision=highest)
        if sweep > 0:
            row_total = lax.psum(row_part, "head")
        else:
            row_total = lax.psum(row_part, "head")
        sample_scale = 1.0 / (total_rows * row_total)
    exp_total = lax.psum(exp_local, "head")
    log_prob = student_raw / student_temp - jnp.log(exp_total)[:, None]
    target = (total_rows * sample_scale)[:, None] * teach_exp * col_scale[None, :]
    loss_part = jnp.sum(target * log_prob)
    grads = (loss_scale * (jnp.exp(log_prob) - target) / student_temp).astype(jnp.bfloat16)
    local_grad = lax.dot_general(
        grads, normed, (((1,), (1,)), ((), ())), preferred_element_type=jnp.float32
    )
    unit_grad = lax.psum(local_grad, "head")
    unit_float = student_unit.astype(jnp.float32)
    row_dot = jnp.sum(unit_float * unit_grad, axis=1, keepdims=True)
    d_rows = inv_norm * (unit_grad - unit_float * row_dot)
    grad_patches = jnp.zeros(student_patches.shape, jnp.float32).at[mask_rows].add(d_rows)
    loss = -lax.psum(loss_part, ("dp", "head")) / total_rows
    slice_rows = prototypes.shape[0] // lax.axis_size("dp")
    normed_grad = lax.psum_scatter(
        lax.dot_general(
            student_unit, grads, (((0,), (0,)), ((), ())), preferred_element_type=jnp.float32
        ),
        "dp",
        scatter_dimension=0,
        tiled=True,
    )
    first_row = lax.axis_index("dp") * slice_rows
    proto_rows = lax.dynamic_slice_in_dim(normed, first_row, slice_rows, 0).astype(jnp.float32)
    col_dot = lax.psum(jnp.sum(proto_rows * normed_grad, axis=0), "dp")
    grad_prototypes = col_inv[None, :] * (normed_grad - proto_rows * col_dot[None, :])
    return (grad_patches, grad_prototypes, loss)


def solution(mesh):
    return jax.shard_map(
        on_device,
        mesh=mesh,
        in_specs=(P("dp", None), P("dp", None), P("dp"), P(None, "head")),
        out_specs=(P("dp", None), P("dp", "head"), P()),
        check_vma=False,
    )
```

profile of v0, /device:TPU:0, one launch (start us, length us, event | category | flops | bytes accessed | tf_op | source)
XLA Modules:
  0.0 625.6 jit_solution(8110453151518073359)
XLA Ops:
  8.0 0.0 copy-start
  8.0 0.0 all-reduce.3.cloned.1.call-start
  8.1 0.7 compare_select_fusion
  8.8 0.7 compare_and_fusion
  9.5 0.0 copy-done
  9.5 2.0 gather_fusion
  11.5 2.7 gather_fusion.1
  14.1 3.1 fusion
  17.2 3.3 fusion.1
  20.6 0.0 copy-start.2
  20.6 0.3 fusion.2
  20.9 2.6 multiply_exponential_fusion
  23.6 0.0 copy-start.1
  23.6 5.7 copy-done.1
  29.3 8.1 %fusion.19 = f32[1,8192]{1,0:T(1,128)S(1)} fusion(f32[512,8192]{1,0:T(8,128)S(1)} %multiply_exponential_fusion), kind=kOutput, calls=%fused_computation.49 | convolution fusion | flops 50331648 | bytes 16809984 | tf_op jit(solution)/shard_map/dot_general | solution.py:42
  37.4 0.0 copy-done.2
  37.4 72.9 %psum.71 = f32[8192]{0:T(1024)S(1)} all-reduce(f32[8192]{0:T(1024)S(1)} %bitcast.32), channel_id=1, replica_groups=mesh['dp'=16,'head'=16] {'dp'}, use_global_device_ids=true, to_apply=%region_5.7 | all-reduce | flops 8192 | bytes 65536 | tf_op jit(solution)/shard_map/psum | solution.py:42
  110.3 17.6 %fusion.28 = f32[1,512]{1,0:T(1,128)S(1)} fusion(f32[512,8192]{1,0:T(8,128)} %copy-done.1, f32[8192,1]{0,1:T(1,128)S(1)} %bitcast.28), kind=kOutput, calls=%fused_computation.55 | convolution fusion | flops 50331648 | bytes 16812032 | tf_op jit(solution)/shard_map/dot_general | solution.py:44
  127.9 26.1 %psum.72 = f32[512]{0:T(512)S(1)} all-reduce(f32[512]{0:T(512)S(1)} %bitcast.34), channel_id=1, replica_groups=mesh['dp'=16,'head'=16] {'head'}, use_global_device_ids=true, to_apply=%region_6.8 | all-reduce | flops 512 | bytes 4096 | tf_op jit(solution)/shard_map/psum | solution.py:48
  154.0 11.5 %fusion.29 = f32[1,8192]{1,0:T(1,128)S(1)} fusion(f32[512,1]{0,1:T(1,128)S(1)} %bitcast.36, f32[512,8192]{1,0:T(8,128)} %copy-done.1), kind=kOutput, calls=%fused_computation.56 | convolution fusion | flops 50331648 | bytes 16812032 | tf_op jit(solution)/shard_map/dot_general | solution.py:42
  165.5 69.7 %psum.73 = f32[8192]{0:T(1024)S(1)} all-reduce(f32[8192]{0:T(1024)S(1)} %bitcast.29), channel_id=1, replica_groups=mesh['dp'=16,'head'=16] {'dp'}, use_global_device_ids=true, to_apply=%region_7.9 | all-reduce | flops 8192 | bytes 65536 | tf_op jit(solution)/shard_map/psum | solution.py:42
  235.2 17.6 %fusion.30 = f32[1,512]{1,0:T(1,128)S(1)} fusion(f32[512,8192]{1,0:T(8,128)} %copy-done.1, f32[8192,1]{0,1:T(1,128)S(1)} %bitcast.30), kind=kOutput, calls=%fused_computation.57 | convolution fusion | flops 50331648 | bytes 16812032 | tf_op jit(solution)/shard_map/dot_general | solution.py:44
  252.8 23.5 %psum.74 = f32[512]{0:T(512)S(1)} all-reduce(f32[512]{0:T(512)S(1)} %bitcast.35), channel_id=1, replica_groups=mesh['dp'=16,'head'=16] {'head'}, use_global_device_ids=true, to_apply=%region_8.10 | all-reduce | flops 512 | bytes 4096 | tf_op jit(solution)/shard_map/psum | solution.py:46
  276.4 11.5 %fusion.31 = f32[1,8192]{1,0:T(1,128)S(1)} fusion(f32[512,1]{0,1:T(1,128)S(1)} %bitcast.37, f32[512,8192]{1,0:T(8,128)} %copy-done.1), kind=kOutput, calls=%fused_computation.58 | convolution fusion | flops 50331648 | bytes 16812032 | tf_op jit(solution)/shard_map/dot_general | solution.py:42
  287.8 69.9 %psum.75 = f32[8192]{0:T(1024)S(1)} all-reduce(f32[8192]{0:T(1024)S(1)} %bitcast.31), channel_id=1, replica_groups=mesh['dp'=16,'head'=16] {'dp'}, use_global_device_ids=true, to_apply=%region_9.11 | all-reduce | flops 8192 | bytes 65536 | tf_op jit(solution)/shard_map/psum | solution.py:42
  357.8 0.0 copy-start.3
  357.8 17.8 %fusion.32 = f32[1,512]{1,0:T(1,128)S(1)} fusion(f32[512,8192]{1,0:T(8,128)} %copy-done.1, f32[8192,1]{0,1:T(1,128)S(1)} %bitcast.27), kind=kOutput, calls=%fused_computation.59 | convolution fusion | flops 50331648 | bytes 16812032 | tf_op jit(solution)/shard_map/dot_general | solution.py:44
  375.6 0.0 copy-done.3
  375.6 7.5 %exponential_reduce_fusion = (f32[512]{0:T(512)S(1)}, f32[512,8192]{1,0:T(8,128)}) fusion(bf16[256,8192]{1,0:T(8,128)(2,1)S(1)} %copy-done.3, f32[512]{0:T(512)S(1)} %get-tuple-element.13, bf16[512,256]{1,0:T(8,128)(2,1)S(1)} %gather_fusion, pred[512]{0:T(512)(128)(4,1)S(1)} %compare_and_fusion), kind=kOutput, calls=%fused_computation.7 | convolution fusion | flops 2156396032 | bytes 21238272 | tf_op jit(solution)/shard_map/dot_general | solution.py:38
  383.0 23.5 %all-reduce = (f32[512]{0:T(512)S(1)}, f32[512]{0:T(512)S(1)}) all-reduce(f32[512]{0:T(512)S(1)} %bitcast.33, f32[512]{0:T(512)S(1)} %get-tuple-element.10), channel_id=1, replica_groups=mesh['dp'=16,'head'=16] {'head'}, use_global_device_ids=true, to_apply=%region_10.12 | all-reduce | flops 1024 | bytes 8192 | tf_op jit(solution)/shard_map/psum | solution.py:46
  406.6 0.0 copy-start.4
  406.6 13.3 %multiply_reduce_fusion = (f32[]{:T(128)}, bf16[512,8192]{1,0:T(8,128)(2,1)S(1)}) fusion(f32[512,8192]{1,0:T(8,128)} %copy-done.1, f32[512,8192]{1,0:T(8,128)} %get-tuple-element.11, f32[8192]{0:T(1024)S(1)} %multiply_divide_fusion, f32[512]{0:T(512)S(1)} %divide_multiply_fusion, f32[512]{0:T(512)S(1)} %log.3), kind=kLoop, calls=%fused_computation.3 | loop fusion | flops 37748736 | bytes 41979908 | tf_op jit(solution)/shard_map/reduce_sum | solution.py:53
  419.8 0.0 copy-start.5
  419.8 3.2 copy-done.5
  423.0 0.0 copy-done.4
  423.0 3.2 fusion.33
  426.2 0.0 all-reduce.3.cloned.1.call-update
  426.2 0.2 reduce-scatter.2.cloned.1.call-start
  426.4 9.1 %fusion.24 = f32[256,8192]{1,0:T(8,128)} fusion(bf16[512,8192]{1,0:T(8,128)(2,1)} %copy-done.5, f32[512]{0:T(512)S(1)} %get-tuple-element.13, bf16[512,256]{1,0:T(8,128)(2,1)S(1)} %gather_fusion, pred[512]{0:T(512)(128)(4,1)S(1)} %compare_and_fusion), kind=kOutput, calls=%fused_computation.53 | convolution fusion | flops 2148007936 | bytes 17041920 | tf_op jit(solution)/shard_map/dot_general | solution.py:66
  435.5 0.0 reduce-scatter.2.cloned.1.call-update
  435.6 73.4 %psum.79 = f32[]{:T(128)} all-reduce(f32[]{:T(128)} %get-tuple-element.8), channel_id=1, replica_groups=mesh['dp'=16,'head'=16] {'dp','head'}, use_global_device_ids=true, to_apply=%region_18.20 | all-reduce | flops 1 | bytes 8 | tf_op jit(solution)/shard_map/psum | solution.py:63
  509.6 23.2 %all-reduce.3.cloned.1.call-done = f32[512,256]{1,0:T(8,128)} async-done(((f32[512,256]{1,0:T(8,128)}), f32[512,256]{1,0:T(8,128)}) %all-reduce.3.cloned.1.call-update) | async-done | bytes 524304 | tf_op jit(solution)/shard_map/psum | solution.py:58
  532.9 1.3 fusion.6
  534.2 5.0 scatter_custom_fusion
  539.3 0.0 reduce-scatter.2.cloned.1.call-done
  539.3 1.2 fusion.11
  540.5 74.4 %psum.78 = f32[8192]{0:T(1024)S(1)} all-reduce(f32[8192]{0:T(1024)S(1)} %fusion.11), channel_id=1, replica_groups=mesh['dp'=16,'head'=16] {'dp'}, use_global_device_ids=true, to_apply=%region_16.18 | all-reduce | flops 8192 | bytes 65536 | tf_op jit(solution)/shard_map/psum | solution.py:75
  614.9 2.0 fusion.13
  (10 shorter events, 0.1 us)
Async XLA Ops:
  8.0 1.5 copy-start
  8.0 524.9 %all-reduce.3.cloned.1.call-start = ((), (), s32[]{:S(2)}) async-start(), calls=%async_computation.1 | async-start | bytes 1048576 | tf_op jit(solution)/shard_map/psum | solution.py:58
  20.6 16.8 %copy-start.2 = (bf16[256,8192]{1,0:T(8,128)(2,1)}, bf16[256,8192]{1,0:T(8,128)(2,1)S(1)}, u32[]{:S(2)}) copy-start(bf16[256,8192]{1,0:T(8,128)(2,1)S(1)} %fusion.1) | copy-start | bytes 12582916
  23.6 5.7 copy-start.1
  357.8 17.8 %copy-start.3 = (bf16[256,8192]{1,0:T(8,128)(2,1)S(1)}, bf16[256,8192]{1,0:T(8,128)(2,1)}, u32[]{:S(2)}) copy-start(bf16[256,8192]{1,0:T(8,128)(2,1)} %copy-done.2) | copy-start | bytes 12582916
  406.6 16.5 %copy-start.4 = (bf16[256,8192]{1,0:T(8,128)(2,1)S(1)}, bf16[256,8192]{1,0:T(8,128)(2,1)}, u32[]{:S(2)}) copy-start(bf16[256,8192]{1,0:T(8,128)(2,1)} %copy-done.2) | copy-start | bytes 12582916
  419.8 3.2 copy-start.5
  426.2 113.0 %reduce-scatter.2.cloned.1.call-start = ((), (), s32[]{:S(2)}) async-start(), calls=%async_computation.2 | async-start | bytes 8912896 | tf_op jit(solution)/shard_map/reduce_scatter | solution.py:65
Sparse Core Ops, SparseCore 0:
  426.3 106.4 all-reduce.2
Sparse Core Ops, SparseCore 1:
  435.7 85.7 reduce-scatter.1
where the time goes:
time: 636 us; the launch traced here: 626 us
  blocking collectives  434 us (68%)
  matrix products  106 us (17%)
  other arithmetic  31.1 us (5%)
  waiting for transfers between devices  23.3 us (4%)
  between operations  17.6 us (3%)
  local copies, waits for them, and re-layouts  13.6 us (2%)
    psum x3, blocking collectives, on_device(): lax.psum(jnp.dot(sample_scale, teach_exp, precision=highest), 'dp')  213 us
    psum x1, blocking collectives, on_device(): col_dot = lax.psum(jnp.sum(proto_rows * normed_grad, axis=0), 'dp')  74.4 us
    psum x1, blocking collectives, on_device(): loss = -lax.psum(loss_part, ('dp', 'head')) / total_rows  73.4 us
    psum x3, blocking collectives, on_device(): row_total = lax.psum(row_part, 'head')  73.2 us
    dot_general x3, matrix products, on_device(): row_part = jnp.dot(teach_exp, col_scale, precision=highest)  53 us
    dot_general x3, matrix products, on_device(): jnp.dot(sample_scale, teach_exp, precision=highest)  31 us
    psum x1, waiting for transfers between devices, on_device(): unit_grad = lax.psum(local_grad, 'head')  23.2 us
    reduce_sum x1, other arithmetic, on_device(): loss_part = jnp.sum(target * log_prob)  13.3 us
  transfers between devices with their start and end apart: 2, of which 1 were waited for; matrix products, arithmetic and copies ran while one was open for 2% of the time, Pallas kernels for 0%

commit v1 on v0

v1 whole, which is shorter than its diff:
```python
import functools
import math

import jax
import jax.numpy as jnp
from jax import lax
from jax.experimental import pallas as pl
from jax.experimental.pallas import tpu as pltpu
from jax.sharding import PartitionSpec as P

MESH = pl.DeviceIdType.MESH
F32, BF16 = jnp.float32, jnp.bfloat16

EPS = 1e-06
LOG2E = math.log2(math.e)
TEACHER = 25.0 * LOG2E
STUDENT = 10.0 * LOG2E
GRAD = 4096.0 / 0.1
ITERS = 3
DP, HEAD, SIDE, DEEP = 16, 16, 4, 8
R, B, C = 512, 256, 8192
W = C // DP
ROWS, K = R * DP, C * HEAD
S = R // HEAD

X0, Y0, H0 = 0, 3, 6
INV, SS, CU, ZU, CP, ZP, AGZ, AGC, A2A, LD, LH = range(9, 20)
SMALL = 20

A1, F1 = lambda u, s: u * 2 + s, lambda u, s: 4 + u * 2 + s
A2, F2 = lambda u, m, s: 8 + (u * 4 + m) * 2 + s, lambda u, m, s: 24 + (u * 4 + m) * 2 + s
MATE = lambda a, b: 40 + a * 4 + b
GATHER = 56
SHIFT = (0, 3, 1, 2)


def nt(a, b):
    return lax.dot_general(a, b, (((1,), (1,)), ((), ())), preferred_element_type=F32)


def nn(a, b):
    return jnp.dot(a, b, preferred_element_type=F32)


def kernel(student, teacher, mask, proto, patch_out, proto_out, loss_out,
           oh, su, tu, invn, nrm, nown, colinv, E, G, ET, suT, PG, TG,
           U, PU, cr, zs, zr, csum, ysum, xr, yr, cs, racc, eacc, sscol,
           hsrc, hr, iva, ssa, agb, a2s, a2r, dhi, dlo, ldr, lhr,
           psend, precv, gsend, grecv, lsem):
    i, j = lax.axis_index("dp"), lax.axis_index("head")
    x, y = i // SIDE, lax.rem(i, SIDE)
    z, c = j // 2, lax.rem(j, 2)
    mate = (i, z * 2 + 1 - c)

    QUARTER = C // 4

    def proto_copy(k):
        cols = pl.ds(k * QUARTER, QUARTER)
        return pltpu.make_async_copy(proto.at[:, cols], nrm.at[:, cols], lsem.at[k])

    for k in range(4):
        proto_copy(k).start()

    barrier = pltpu.get_barrier_semaphore()
    for d in range(1, DP):
        pl.semaphore_signal(barrier, inc=1, device_id=(lax.rem(i + d, DP), j), device_id_type=MESH)
        pl.semaphore_signal(barrier, inc=1, device_id=(i, lax.rem(j + d, HEAD)), device_id_type=MESH)

    def send(src, dst, ph, dev):
        pltpu.make_async_remote_copy(src, dst, psend.at[ph], precv.at[ph], device_id=dev, device_id_type=MESH).start()

    def landed(like, ph):
        pltpu.make_async_copy(like, like, precv.at[ph]).wait()

    def sent(like, ph):
        pltpu.make_async_copy(like, like, psend.at[ph]).wait()

    def along_x(d):
        return (lax.rem(x + d, SIDE) * SIDE + y, j)

    def along_y(d):
        return (x * SIDE + lax.rem(y + d, SIDE), j)

    def along_dp(d):
        return (lax.rem(i + d, DP), j)

    def along_head(d):
        return (i, lax.rem(j + d, HEAD))

    def along_z(d):
        return (i, lax.rem(z + d, DEEP) * 2 + c)

    p = x * (1 - c) + y * c
    q = y * (1 - c) + x * c

    def at(dp_, dq_):
        pp, qq = lax.rem(p + dp_, SIDE), lax.rem(q + dq_, SIDE)
        return (pp * SIDE + qq) * (1 - c) + (qq * SIDE + pp) * c

    HALF = R // 4

    def part(blk, u, half=None):
        if half is None:
            return G.at[blk, c, u]
        return G.at[blk, c, u, pl.ds(half * HALF, HALF)]

    def gcopy(ref, sid, dev):
        return pltpu.make_async_remote_copy(ref, ref, gsend.at[sid], grecv.at[sid], device_id=dev, device_id_type=MESH)

    def gwait(ref, sid):
        pltpu.make_async_copy(ref, ref, grecv.at[sid]).wait()

    def n1(s):
        return (at(1 if s == 0 else 3, 0), j)

    def n2(s):
        return (at(0, 1 if s == 0 else 3), j)

    def a1_send(u):
        for s in (0, 1):
            gcopy(part(at(0, 0), u), A1(u, s), n1(s)).start()

    def a1_wait(u):
        for s in (0, 1):
            gwait(part(at(3 if s == 0 else 1, 0), u), A1(u, s))

    def f1_send(u):
        for s in (0, 1):
            gcopy(part(at(3 if s == 0 else 1, 0), u, s), F1(u, s), n1(s)).start()

    def f1_wait(u):
        for s in (0, 1):
            gwait(part(at(2, 0), u, s), F1(u, s))

    def a2_send(u, m):
        for s in (0, 1):
            gcopy(part(at(SHIFT[m], 0), u), A2(u, m, s), n2(s)).start()

    def a2_wait(u, m):
        for s in (0, 1):
            gwait(part(at(SHIFT[m], 3 if s == 0 else 1), u), A2(u, m, s))

    def f2_send(u, m):
        for s in (0, 1):
            gcopy(part(at(SHIFT[m], 3 if s == 0 else 1), u, s), F2(u, m, s), n2(s)).start()

    def f2_wait(u, m):
        for s in (0, 1):
            gwait(part(at(SHIFT[m], 2), u, s), F2(u, m, s))

    def mate_send(a, b):
        ref = G.at[at(a, b), c]
        pltpu.make_async_remote_copy(ref, ref, gsend.at[MATE(a, b)], grecv.at[MATE(a, b)], device_id=mate, device_id_type=MESH).start()

    def mate_wait(a, b):
        ref = G.at[at(a, b), 1 - c]
        pltpu.make_async_copy(ref, ref, grecv.at[MATE(b, a)]).wait()

    def slot(n):
        if n == 0:
            a1_send(0)
            a2_send(0, 0)
        elif n == 1:
            a1_send(1)
            a2_send(1, 0)
        elif n in (2, 3):
            u = n - 2
            a1_wait(u)
            f1_send(u)
            a2_wait(u, 0)
            f2_send(u, 0)
            a2_send(u, 1)
            if u == 1:
                for a, b in ((1, 0), (3, 0), (0, 1), (0, 3)):
                    mate_send(a, b)
        elif n in (4, 5):
            u = n - 4
            a2_wait(u, 1)
            f2_send(u, 1)
            a2_send(u, 2)
            f1_wait(u)
            f2_wait(u, 0)
            if u == 1:
                for a, b in ((2, 0), (0, 2), (3, 1), (3, 3)):
                    mate_send(a, b)
        elif n in (6, 7):
            u = n - 6
            a2_wait(u, 2)
            f2_send(u, 2)
            a2_send(u, 3)
            f2_wait(u, 1)
            if u == 1:
                for a, b in ((3, 2), (1, 1), (1, 3)):
                    mate_send(a, b)
        elif n == 8:
            a2_wait(0, 3)
            f2_send(0, 3)
            a2_wait(1, 3)
            f2_send(1, 3)
            f2_wait(0, 2)
            f2_wait(1, 2)
            for a, b in ((2, 1), (2, 3), (1, 2)):
                mate_send(a, b)
        elif n == 9:
            f2_wait(0, 3)
            f2_wait(1, 3)
            mate_send(2, 2)

    @pl.loop(0, 8)
    def _(k):
        rows = pl.ds(pl.multiple_of(k * 128, 128), 128)
        patch = lax.broadcasted_iota(jnp.int32, (128, R), 0) + k * 128
        oh[rows, :] = jnp.where(patch == mask[...], 1.0, 0.0).astype(BF16)

    def unit(patches):
        rows = lax.dot_general(oh[...], patches[...], (((0,), (0,)), ((), ())), preferred_element_type=F32)
        inverse = lax.rsqrt(jnp.sum(rows * rows, axis=1, keepdims=True) + EPS)
        return (rows * inverse).astype(BF16), inverse

    unit_s, inv_s = unit(student)
    su[...] = unit_s
    invn[...] = jnp.broadcast_to(inv_s, (R, 128))
    unit_t, _ = unit(teacher)
    tu[...] = unit_t
    for half in (0, 1):
        rows = slice(half * (R // 2), (half + 1) * (R // 2))
        G[i, half, 0] = su[rows, :].astype(F32)
        G[i, half, 1] = tu[rows, :].astype(F32)

    pl.semaphore_wait(barrier, DP + HEAD - 2)
    slot(0)

    for k in range(4):
        proto_copy(k).wait()

    @pl.loop(0, C // W)
    def _(k):
        cols = pl.ds(pl.multiple_of(k * W, W), W)
        w = nrm[:, cols].astype(F32)
        inverse = lax.rsqrt(jnp.sum(w * w, axis=0, keepdims=True) + EPS)
        n = (w * inverse).astype(BF16)
        colinv[:, cols] = inverse
        nrm[:, cols] = n
        e = jnp.exp2(nn(tu[...], n) * TEACHER)
        E[:, cols] = e
        csum[0, :, cols] = jnp.sum(e, axis=0, keepdims=True)

    mine = pl.ds(pl.multiple_of(i * W, W), W)
    nown[...] = nrm[:, mine]
    PU[...] = jnp.zeros_like(PU)
    U[...] = jnp.zeros_like(U)
    PG[...] = jnp.zeros_like(PG)
    TG[...] = jnp.zeros_like(TG)
    eacc[...] = jnp.zeros_like(eacc)

    def tiles(v):
        total = v[:, 0:128]
        for t in range(1, v.shape[1] // 128):
            total = total + v[:, t * 128:(t + 1) * 128]
        return total

    def student_chunks(first, last):
        @pl.loop(first, last)
        def _(k):
            cols = pl.ds(pl.multiple_of(k * W, W), W)
            n = nrm[:, cols]
            e = jnp.exp2(nn(su[...], n) * STUDENT)
            eacc[...] += tiles(e)
            PU[...] += nt(e.astype(BF16), n).reshape(DEEP, 2, S, B)

    def across(v):
        return jnp.sum(v.T, axis=0, keepdims=True)

    def down(v):
        return jnp.broadcast_to(v, (128, R)).T

    def row_pass():
        @pl.loop(0, R // 64)
        def _(k):
            rows = pl.ds(pl.multiple_of(k * 64, 64), 64)
            total = jnp.zeros((64, 128), F32)
            for t in range(C // 128):
                total = total + E[rows, t * 128:(t + 1) * 128] * cs[:, t * 128:(t + 1) * 128]
            racc[rows, :] = total

    def last_row_pass():
        racc[...] = jnp.zeros_like(racc)

        @pl.loop(0, C // W)
        def _(k):
            cols = pl.ds(pl.multiple_of(k * W, W), W)
            t = E[:, cols] * cs[:, cols]
            racc[...] += tiles(t)
            U[...] += nt(t.astype(BF16), nrm[:, cols]).reshape(DEEP, 2, S, B)

    def col_pass(it):
        @pl.loop(0, C // 1024)
        def _(k):
            cols = pl.ds(pl.multiple_of(k * 1024, 1024), 1024)
            total = jnp.zeros((8, 1024), F32)
            for r in range(R // 8):
                scale = sscol[r * 8:(r + 1) * 8, :]
                total = total + E[r * 8:(r + 1) * 8, cols] * jnp.concatenate([scale] * 8, axis=1)
            csum[it, :, cols] = jnp.sum(total, axis=0, keepdims=True)

    def block(a, b):
        blk = at(a, b)
        s = G[blk, :, 0].reshape(R, B).astype(BF16)
        t = G[blk, :, 1].reshape(R, B).astype(BF16)
        ET[blk] = jnp.exp2(nn(t, nown[...]) * TEACHER).astype(BF16)
        e = jnp.exp2(nn(s, nown[...]) * STUDENT).astype(BF16)
        turned = s.astype(F32).T
        suT[blk] = turned.astype(BF16)
        PG[...] += nn((turned * iva[blk]).astype(BF16), e)

    def blocks(pairs):
        for a, b in pairs:
            if (a, b) != (0, 0):
                mate_wait(a, b)
            block(a, b)

    def core_sum_send(v, which, ph):
        send(v.at[:, 1 - c], cr.at[which], ph, mate)

    def core_sum_wait(v, which, ph, zph):
        landed(cr.at[which], ph)
        zs[which] = v[:, c] + cr[which]
        for d in range(1, DEEP):
            send(zs.at[which, lax.rem(z + d, DEEP)], zr.at[which, d - 1], zph, along_z(d))

    def z_sum(which, zph):
        landed(zr.at[which], zph)
        total = zs[which, z]
        for d in range(DEEP - 1):
            total = total + zr[which, d]
        return total

    for it in range(ITERS):
        for d in range(1, SIDE):
            send(csum.at[it], xr.at[it, d - 1], X0 + it, along_x(d))
        slot(3 * it + 1)
        if it == 0:
            student_chunks(0, 5)
        elif it == 1:
            landed(iva.at[pl.ds(0, DP - 1)], INV)
            blocks(((0, 0),))
            core_sum_wait(PU, 0, CP, ZP)
        elif it == 2:
            blocks(((0, 2), (3, 1), (3, 3)))
        landed(xr.at[it], X0 + it)
        ysum[it] = csum[it] + xr[it, 0] + xr[it, 1] + xr[it, 2]
        for d in range(1, SIDE):
            send(ysum.at[it], yr.at[it, d - 1], Y0 + it, along_y(d))
        slot(3 * it + 2)
        if it == 0:
            student_chunks(5, 16)
        elif it == 1:
            blocks(((1, 0), (3, 0), (0, 1)))
        elif it == 2:
            blocks(((3, 2), (1, 1), (1, 3)))
        landed(yr.at[it], Y0 + it)
        cs[...] = 1.0 / (K * (ysum[it] + yr[it, 0] + yr[it, 1] + yr[it, 2]))
        if it < ITERS - 1:
            row_pass()
        else:
            last_row_pass()
            core_sum_send(U, 1, CU)
        hsrc[it, :, 0:R] = across(racc[...])
        if it == 0:
            hsrc[it, :, R:2 * R] = across(eacc[...])
        wide = 2 * R if it == 0 else R
        for d in range(1, HEAD):
            send(hsrc.at[it, :, pl.ds(0, wide)], hr.at[it, d - 1, :, pl.ds(0, wide)], H0 + it, along_head(d))
        slot(3 * it + 3)
        if it == 0:
            core_sum_send(PU, 0, CP)
        elif it == 1:
            blocks(((0, 3), (2, 0)))
        elif it == 2:
            core_sum_wait(U, 1, CU, ZU)
        landed(hr.at[it, :, :, pl.ds(0, wide)], H0 + it)
        row_total = hsrc[it, :, 0:R]
        for d in range(HEAD - 1):
            row_total = row_total + hr[it, d, :, 0:R]
        if it == 0:
            exp_total = hsrc[it, :, R:2 * R]
            for d in range(HEAD - 1):
                exp_total = exp_total + hr[it, d, :, R:2 * R]
            iva[i] = 1.0 / exp_total
            for d in range(1, DP):
                send(iva.at[i], iva.at[i], INV, along_dp(d))
        if it < ITERS - 1:
            sscol[...] = down(1.0 / (ROWS * row_total))
            col_pass(it + 1)

    ssa[i] = 1.0 / row_total
    for d in range(1, DP):
        send(ssa.at[i], ssa.at[i], SS, along_dp(d))
    blocks(((2, 1), (2, 3), (1, 2), (2, 2)))
    landed(ssa.at[pl.ds(0, DP - 1)], SS)

    @pl.loop(0, DP)
    def _(k):
        TG[...] += nn((suT[k].astype(F32) * ssa[k]).astype(BF16), ET[k])

    unit_cols = nown[...].astype(F32)
    normed_grad = GRAD * (PG[...] - cs[:, mine] * TG[...])
    col_dot = jnp.sum(unit_cols * normed_grad, axis=0, keepdims=True)
    a2s[...] = (colinv[:, mine] * (normed_grad - unit_cols * col_dot)).reshape(DP, B // DP, W)
    for d in range(1, DP):
        send(a2s.at[lax.rem(i + d, DP)], a2r.at[i], A2A, along_dp(d))
    a2r[i] = a2s[i]

    target_sum = z_sum(1, ZU)
    student_sum = z_sum(0, ZP)
    own = lax.broadcasted_iota(jnp.int32, (S, R), 1) == lax.broadcasted_iota(jnp.int32, (S, R), 0) + j * S

    def pick(v):
        return jnp.sum(jnp.where(own, v, 0.0), axis=1, keepdims=True)

    own_rows = pl.ds(pl.multiple_of(j * S, S), S)
    in_half = pl.ds(pl.multiple_of(lax.rem(j, 8) * S, S), S)
    unit_rows = G[i, j // 8, 0, in_half]
    target_mean = target_sum * pick(ssa[i])
    exp_inv = pick(iva[i])
    unit_grad = GRAD * (student_sum * exp_inv - target_mean)
    row_dot = jnp.sum(unit_rows * unit_grad, axis=1, keepdims=True)
    agb[c, z] = invn[own_rows, 0:1] * (unit_grad - unit_rows * row_dot)
    for d in range(1, DEEP):
        send(agb.at[c, z], agb.at[c, z], AGZ, along_z(d))
    raw_mean = jnp.sum(unit_rows * target_mean, axis=1, keepdims=True)
    part_loss = jnp.sum(raw_mean * 10.0 + jnp.log(exp_inv), axis=0, keepdims=True)
    ldr[i] = jnp.broadcast_to(part_loss, (1, 128))
    for d in range(1, DP):
        send(ldr.at[i], ldr.at[i], LD, along_dp(d))

    landed(agb.at[c, pl.ds(0, DEEP - 1)], AGZ)
    send(agb.at[c], agb.at[c], AGC, mate)
    landed(a2r.at[pl.ds(0, DP - 1)], A2A)
    for d in range(DP):
        proto_out[:, d * W:(d + 1) * W] = a2r[d]
    landed(ldr.at[pl.ds(0, DP - 1)], LD)
    total = ldr[0]
    for d in range(1, DP):
        total = total + ldr[d]
    lhr[j] = total
    for d in range(1, HEAD):
        send(lhr.at[j], lhr.at[j], LH, along_head(d))

    landed(agb.at[1 - c], AGC)
    for k in range(DEEP):
        for h in (0, 1):
            rows = slice((k * 2 + h) * S, (k * 2 + h + 1) * S)
            v = agb[h, k]
            high = v.astype(BF16)
            dhi[rows, :] = high
            dlo[rows, :] = (v - high.astype(F32)).astype(BF16)

    @pl.loop(0, 4)
    def _(k):
        rows = pl.ds(pl.multiple_of(k * 256, 256), 256)
        patch_out[rows, :] = nn(oh[rows, :], dhi[...]) + nn(oh[rows, :], dlo[...])

    landed(lhr.at[pl.ds(0, HEAD - 1)], LH)
    total = lhr[0]
    for d in range(1, HEAD):
        total = total + lhr[d]
    loss_out[...] = total * (-1.0 / ROWS)

    for it in range(ITERS):
        sent(xr.at[it], X0 + it)
        sent(yr.at[it], Y0 + it)
        wide = 2 * R if it == 0 else R
        sent(hr.at[it, :, :, pl.ds(0, wide)], H0 + it)
    sent(iva.at[pl.ds(0, DP - 1)], INV)
    sent(ssa.at[pl.ds(0, DP - 1)], SS)
    sent(cr.at[1], CU)
    sent(cr.at[0], CP)
    sent(zr.at[1], ZU)
    sent(zr.at[0], ZP)
    sent(agb.at[c, pl.ds(0, DEEP - 1)], AGZ)
    sent(agb.at[c], AGC)
    sent(a2r.at[pl.ds(0, DP - 1)], A2A)
    sent(ldr.at[pl.ds(0, DP - 1)], LD)
    sent(lhr.at[pl.ds(0, HEAD - 1)], LH)
    whole, half = part(i, 0), part(i, 0, 0)

    def gsent(like, sid):
        pltpu.make_async_copy(like, like, gsend.at[sid]).wait()

    for u in (0, 1):
        for s in (0, 1):
            gsent(whole, A1(u, s))
            gsent(half, F1(u, s))
            for m in range(4):
                gsent(whole, A2(u, m, s))
                gsent(half, F2(u, m, s))
    for a in range(SIDE):
        for b in range(SIDE):
            if (a, b) != (0, 0):
                gsent(G.at[i, c], MATE(a, b))


def on_device(student_patches, teacher_patches, mask_rows, prototypes):
    vm = pltpu.VMEM
    whole = pl.BlockSpec(memory_space=pltpu.VMEM)
    patches, protos, loss = pl.pallas_call(
        kernel,
        out_shape=(
            jax.ShapeDtypeStruct(student_patches.shape, F32),
            jax.ShapeDtypeStruct((B // DP, C), F32),
            jax.ShapeDtypeStruct((1, 128), F32),
        ),
        in_specs=[whole] * 3 + [pl.BlockSpec(memory_space=pl.ANY)],
        out_specs=(whole, whole, whole),
        scratch_shapes=[
            vm((1024, R), BF16),
            vm((R, B), BF16),
            vm((R, B), BF16),
            vm((R, 128), F32),
            vm((B, C), BF16),
            vm((B, W), BF16),
            vm((1, C), F32),
            vm((R, C), F32),
            vm((DP, 2, 2, R // 2, B), F32),
            vm((DP, R, W), BF16),
            vm((DP, B, R), BF16),
            vm((B, W), F32),
            vm((B, W), F32),
            vm((DEEP, 2, S, B), F32),
            vm((DEEP, 2, S, B), F32),
            vm((2, DEEP, S, B), F32),
            vm((2, DEEP, S, B), F32),
            vm((2, DEEP - 1, S, B), F32),
            vm((ITERS, 1, C), F32),
            vm((ITERS, 1, C), F32),
            vm((ITERS, SIDE - 1, 1, C), F32),
            vm((ITERS, SIDE - 1, 1, C), F32),
            vm((1, C), F32),
            vm((R, 128), F32),
            vm((R, 128), F32),
            vm((R, 128), F32),
            vm((ITERS, 1, 2 * R), F32),
            vm((ITERS, HEAD - 1, 1, 2 * R), F32),
            vm((DP, 1, R), F32),
            vm((DP, 1, R), F32),
            vm((2, DEEP, S, B), F32),
            vm((DP, B // DP, W), F32),
            vm((DP, B // DP, W), F32),
            vm((R, B), BF16),
            vm((R, B), BF16),
            vm((DP, 1, 128), F32),
            vm((HEAD, 1, 128), F32),
            pltpu.SemaphoreType.DMA((SMALL,)),
            pltpu.SemaphoreType.DMA((SMALL,)),
            pltpu.SemaphoreType.DMA((GATHER,)),
            pltpu.SemaphoreType.DMA((GATHER,)),
            pltpu.SemaphoreType.DMA((4,)),
        ],
        compiler_params=pltpu.CompilerParams(
            collective_id=0, has_side_effects=True, vmem_limit_bytes=63 * 2**20
        ),
    )(student_patches, teacher_patches, mask_rows.reshape(1, R), prototypes)
    return patches, protos, loss[0, 0]


def solution(mesh):
    return jax.shard_map(
        on_device,
        mesh=mesh,
        in_specs=(P("dp", None), P("dp", None), P("dp"), P(None, "head")),
        out_specs=(P("dp", None), P("dp", "head"), P()),
        check_vma=False,
    )
```

time: 636 us -> 108 us (0.17)
  the two profiles are of different devices: /device:TPU:0 before, /device:TPU:1 now
where the time goes in v1:
time: 108 us
  Pallas kernels  102 us (94%)
  local copies, waits for them, and re-layouts  4.13 us (4%)
  between operations  2.41 us (2%)
    pallas_call x1, Pallas kernels, on_device(): pl.pallas_call(kernel, out_shape=(jax.ShapeDtypeStruct(student_patches.sh...  102 us
    unnamed x2, local copies, waits for them, and re-layouts  4.13 us

profile of v1, /device:TPU:1, one launch (start us, length us, event | category | flops | bytes accessed | tf_op | source)
XLA Modules:
  0.0 108.1 jit_solution(4739865541191151840)
XLA Ops:
  0.6 101.5 %shard_map.67 = (f32[1024,256]{1,0:T(8,128)}, f32[16,8192]{1,0:T(8,128)}, f32[1,128]{1,0:T(1,128)}) custom-call(bf16[1024,256]{1,0:T(8,128)(2,1)} %student.1, bf16[1024,256]{1,0:T(8,128)(2,1)} %teacher.1, s32[1,512]{1,0:T(1,128)} %bitcast.3, bf16[256,8192]{1,0:T(8,128)(2,1)} %proto.1), custom_call_target="tpu_custom_call" | custom-call | tf_op jit(solution)/shard_map/pallas_call | solution.py:507
  102.2 2.3 %copy.10 = f32[1024,256]{1,0:T(8,128)} copy(f32[1024,256]{1,0:T(8,128)} %get-tuple-element.12) | data formatting | bytes 2097152
  104.4 1.9 %copy.11 = f32[16,8192]{1,0:T(8,128)} copy(f32[16,8192]{1,0:T(8,128)} %get-tuple-element.13) | data formatting | bytes 1048576

commit v2 on v1

v2 whole, which is shorter than its diff:
```python
import functools
import math

import jax
import jax.numpy as jnp
from jax import lax
from jax.experimental import pallas as pl
from jax.experimental.pallas import tpu as pltpu
from jax.sharding import PartitionSpec as P

MESH = pl.DeviceIdType.MESH
F32, BF16 = jnp.float32, jnp.bfloat16

EPS = 1e-06
LOG2E = math.log2(math.e)
TEACHER = 25.0 * LOG2E
STUDENT = 10.0 * LOG2E
GRAD = 4096.0 / 0.1
ITERS = 3
DP, HEAD, SIDE, DEEP = 16, 16, 4, 8
R, B, C = 512, 256, 8192
W = C // DP
ROWS, K = R * DP, C * HEAD
S = R // HEAD

CH = 4
CW = C // CH
LAST_W = 1024
X0, Y0, H0 = 0, ITERS * CH, 2 * ITERS * CH
INV, SS, CU, ZU, CP, ZP, AGZ, AGC, LD, LH, A2A = range(H0 + ITERS, H0 + ITERS + 11)
SMALL = A2A + 2


def far_first(sides):
    offsets = [(a, b) for a in range(sides[0]) for b in range(sides[1]) if (a, b) != (0, 0)]
    return sorted(offsets, key=lambda o: -min(o[0], sides[0] - o[0]) - min(o[1], sides[1] - o[1]))


DP_OFF, HEAD_OFF = far_first((SIDE, SIDE)), far_first((DEEP, 2))

A1, F1 = lambda u, s: u * 2 + s, lambda u, s: 4 + u * 2 + s
A2, F2 = lambda u, m, s: 8 + (u * 4 + m) * 2 + s, lambda u, m, s: 24 + (u * 4 + m) * 2 + s
MATE = lambda a, b: 40 + a * 4 + b
ZED = lambda a, b, s: 56 + (a * 4 + b) * 2 + s
GATHER = 88
PLANE, BESIDE = 176, 80
SHIFT = (0, 3, 1, 2)


def nt(a, b):
    return lax.dot_general(a, b, (((1,), (1,)), ((), ())), preferred_element_type=F32)


def nn(a, b):
    return jnp.dot(a, b, preferred_element_type=F32)


def kernel(student, teacher, mask, proto, patch_out, proto_out, loss_out,
           oh, su, tu, invn, nrm, nown, colinv, E, G, ET, suT, PG,
           U, PU, cr, zs, zr, csum, ysum, xr, yr, cs, racc, eacc, sscol,
           hsrc, hr, iva, ssa, agb, a2s, a2r, wide_out, dhi, dlo, ldr, lhr,
           psend, precv, gsend, grecv, lsem, osem):
    i, j = lax.axis_index("dp"), lax.axis_index("head")
    x, y = i // SIDE, lax.rem(i, SIDE)
    z, c = j // 2, lax.rem(j, 2)
    mate = (i, z * 2 + 1 - c)

    def proto_copy(k):
        cols = pl.ds(k * CW, CW)
        return pltpu.make_async_copy(proto.at[:, cols], nrm.at[:, cols], lsem.at[k])

    for k in range(CH):
        proto_copy(k).start()

    barrier = pltpu.get_barrier_semaphore()
    for d in range(1, DP):
        pl.semaphore_signal(barrier, inc=1, device_id=(lax.rem(i + d, DP), j), device_id_type=MESH)
        pl.semaphore_signal(barrier, inc=1, device_id=(i, lax.rem(j + d, HEAD)), device_id_type=MESH)

    def send(src, dst, ph, dev):
        pltpu.make_async_remote_copy(src, dst, psend.at[ph], precv.at[ph], device_id=dev, device_id_type=MESH).start()

    def landed(like, ph):
        pltpu.make_async_copy(like, like, precv.at[ph]).wait()

    def sent(like, ph):
        pltpu.make_async_copy(like, like, psend.at[ph]).wait()

    def along_x(d):
        return (lax.rem(x + d, SIDE) * SIDE + y, j)

    def along_y(d):
        return (x * SIDE + lax.rem(y + d, SIDE), j)

    def to_dp(src, dst, ph):
        for a, b in DP_OFF:
            send(src, dst, ph, (lax.rem(x + a, SIDE) * SIDE + lax.rem(y + b, SIDE), j))

    def to_head(src, dst, ph):
        for e, (a, b) in enumerate(HEAD_OFF):
            send(src, dst(e), ph, (i, lax.rem(z + a, DEEP) * 2 + lax.rem(c + b, 2)))

    def along_z(d):
        return (i, lax.rem(z + d, DEEP) * 2 + c)

    p = x * (1 - c) + y * c
    q = y * (1 - c) + x * c

    def at(dp_, dq_):
        pp, qq = lax.rem(p + dp_, SIDE), lax.rem(q + dq_, SIDE)
        return (pp * SIDE + qq) * (1 - c) + (qq * SIDE + pp) * c

    odd = lax.rem(z, 2)

    def part(blk, u, half=None):
        first = odd * BESIDE + (0 if half is None else half * (PLANE // 2))
        rows = pl.ds(pl.multiple_of(first, 8), PLANE if half is None else PLANE // 2)
        return G.at[blk, c, u, rows]

    def beside(blk, which, s):
        first = which * PLANE + s * (BESIDE // 2)
        return G.at[blk, c, :, pl.ds(pl.multiple_of(first, 8), BESIDE // 2)]

    def z_send(pairs):
        for a, b in pairs:
            for s in (0, 1):
                gcopy(beside(at(a, b), odd, s), ZED(a, b, s), along_z(1 if s == 0 else DEEP - 1)).start()

    def gcopy(ref, sid, dev):
        return pltpu.make_async_remote_copy(ref, ref, gsend.at[sid], grecv.at[sid], device_id=dev, device_id_type=MESH)

    def gwait(ref, sid):
        pltpu.make_async_copy(ref, ref, grecv.at[sid]).wait()

    def n1(s):
        return (at(1 if s == 0 else 3, 0), j)

    def n2(s):
        return (at(0, 1 if s == 0 else 3), j)

    def a1_send(u):
        for s in (0, 1):
            gcopy(part(at(0, 0), u), A1(u, s), n1(s)).start()

    def a1_wait(u):
        for s in (0, 1):
            gwait(part(at(3 if s == 0 else 1, 0), u), A1(u, s))

    def f1_send(u):
        for s in (0, 1):
            gcopy(part(at(3 if s == 0 else 1, 0), u, s), F1(u, s), n1(s)).start()

    def f1_wait(u):
        for s in (0, 1):
            gwait(part(at(2, 0), u, s), F1(u, s))

    def a2_send(u, m):
        for s in (0, 1):
            gcopy(part(at(SHIFT[m], 0), u), A2(u, m, s), n2(s)).start()

    def a2_wait(u, m):
        for s in (0, 1):
            gwait(part(at(SHIFT[m], 3 if s == 0 else 1), u), A2(u, m, s))

    def f2_send(u, m):
        for s in (0, 1):
            gcopy(part(at(SHIFT[m], 3 if s == 0 else 1), u, s), F2(u, m, s), n2(s)).start()

    def f2_wait(u, m):
        for s in (0, 1):
            gwait(part(at(SHIFT[m], 2), u, s), F2(u, m, s))

    def mate_send(pairs):
        for a, b in pairs:
            for s in (0, 1):
                gwait(beside(at(a, b), 1 - odd, s), ZED(a, b, s))
            gcopy(G.at[at(a, b), c], MATE(a, b), mate).start()

    def mate_wait(a, b):
        ref = G.at[at(a, b), 1 - c]
        pltpu.make_async_copy(ref, ref, grecv.at[MATE(b, a)]).wait()

    NEAR = ((1, 0), (3, 0), (0, 1), (0, 3))
    MID = ((2, 0), (0, 2), (3, 1), (3, 3))
    FAR = ((3, 2), (1, 1), (1, 3))
    LAST = ((2, 1), (2, 3), (1, 2))
    END = ((2, 2),)
    READY_MID = ((2, 0), (0, 2), (3, 3))
    READY_FAR = ((3, 1), (1, 1), (1, 3))
    READY_LAST = ((2, 3), (3, 2), (1, 2), (2, 1), (2, 2))

    def slot(n):
        if n in (0, 1):
            a1_send(n)
            a2_send(n, 0)
        elif n in (2, 3):
            u = n - 2
            a1_wait(u)
            f1_send(u)
            a2_wait(u, 0)
            f2_send(u, 0)
            a2_send(u, 1)
            if u == 1:
                z_send(NEAR)
        elif n == 4:
            a2_wait(0, 1)
            f2_send(0, 1)
            a2_send(0, 2)
            a2_send(1, 2)
            f1_wait(0)
            f2_wait(0, 0)
        elif n == 5:
            a2_wait(1, 1)
            f2_send(1, 1)
            f1_wait(1)
            a2_send(0, 3)
            a2_send(1, 3)
            f2_wait(1, 0)
            mate_send(NEAR)
            z_send(MID)
        elif n == 6:
            for u in (0, 1):
                a2_wait(u, 2)
                f2_send(u, 2)
                f2_wait(u, 1)
            z_send(FAR)
        elif n == 7:
            for u in (0, 1):
                a2_wait(u, 3)
                f2_send(u, 3)
            mate_send(MID)
        elif n == 8:
            f2_wait(0, 3)
            f2_wait(1, 3)
            z_send(END)
            mate_send(FAR)

    def late_slot():
        f2_wait(0, 2)
        f2_wait(1, 2)
        z_send(LAST)

    @pl.loop(0, 8)
    def _(k):
        rows = pl.ds(pl.multiple_of(k * 128, 128), 128)
        patch = lax.broadcasted_iota(jnp.int32, (128, R), 0) + k * 128
        oh[rows, :] = jnp.where(patch == mask[...], 1.0, 0.0).astype(BF16)

    def unit(patches):
        rows = lax.dot_general(oh[...], patches[...], (((0,), (0,)), ((), ())), preferred_element_type=F32)
        inverse = lax.rsqrt(jnp.sum(rows * rows, axis=1, keepdims=True) + EPS)
        return (rows * inverse).astype(BF16), inverse

    unit_s, inv_s = unit(student)
    su[...] = unit_s
    invn[...] = jnp.broadcast_to(inv_s, (R, 128))
    unit_t, _ = unit(teacher)
    tu[...] = unit_t
    for half in (0, 1):
        rows = slice(half * (R // 2), (half + 1) * (R // 2))
        G[i, half, 0] = su[rows, :].astype(F32)
        G[i, half, 1] = tu[rows, :].astype(F32)

    def x_send(it, k):
        for d in (2, 1, 3):
            send(csum.at[it, k], xr.at[it, k, d - 1], X0 + it * CH + k, along_x(d))

    for k in range(CH):
        proto_copy(k).wait()

        for n in range(CW // W):
            cols = slice(k * CW + n * W, k * CW + (n + 1) * W)
            w = nrm[:, cols].astype(F32)
            inverse = lax.rsqrt(jnp.sum(w * w, axis=0, keepdims=True) + EPS)
            unit_cols = (w * inverse).astype(BF16)
            colinv[:, cols] = inverse
            nrm[:, cols] = unit_cols
            e = jnp.exp2(nn(tu[...], unit_cols) * TEACHER)
            E[:, cols] = e
            csum[0, k, :, n * W:(n + 1) * W] = jnp.sum(e, axis=0, keepdims=True)

        if k == 2:
            pl.semaphore_wait(barrier, DP + HEAD - 2)
            for n in range(3):
                x_send(0, n)
    x_send(0, 3)

    mine = pl.ds(pl.multiple_of(i * W, W), W)
    nown[...] = nrm[:, mine]
    PU[...] = jnp.zeros_like(PU)
    U[...] = jnp.zeros_like(U)
    PG[...] = jnp.zeros_like(PG)
    eacc[...] = jnp.zeros_like(eacc)

    def tiles(v):
        total = v[:, 0:128]
        for t in range(1, v.shape[1] // 128):
            total = total + v[:, t * 128:(t + 1) * 128]
        return total

    def student_chunks(first, last):
        @pl.loop(first // 4, last // 4)
        def _(k):
            for n in range(4):
                cols = pl.ds(pl.multiple_of(k * 4 * W + n * W, W), W)
                unit_cols = nrm[:, cols]
                e = jnp.exp2(nn(su[...], unit_cols) * STUDENT)
                eacc[...] += tiles(e)
                PU[...] += nt(e.astype(BF16), unit_cols).reshape(DEEP, 2, S, B)

    def across(v):
        return jnp.sum(v.T, axis=0, keepdims=True)

    def down(v):
        return jnp.broadcast_to(v, (128, R)).T

    def y_step(it, k):
        landed(xr.at[it, k], X0 + it * CH + k)
        ysum[it, k] = csum[it, k] + xr[it, k, 0] + xr[it, k, 1] + xr[it, k, 2]
        for d in (2, 1, 3):
            send(ysum.at[it, k], yr.at[it, k, d - 1], Y0 + it * CH + k, along_y(d))

    def row_step(it, k):
        landed(yr.at[it, k], Y0 + it * CH + k)
        cs[:, k * CW:(k + 1) * CW] = 1.0 / (K * (ysum[it, k] + yr[it, k, 0] + yr[it, k, 1] + yr[it, k, 2]))
        if it < ITERS - 1:
            @pl.loop(0, R // 64)
            def _(n):
                rows = pl.ds(pl.multiple_of(n * 64, 64), 64)
                total = jnp.zeros((64, 128), F32) if k == 0 else racc[rows, :]
                for t in range(k * CW // 128, (k + 1) * CW // 128):
                    total = total + E[rows, t * 128:(t + 1) * 128] * cs[:, t * 128:(t + 1) * 128]
                racc[rows, :] = total

    def last_pass():
        racc[...] = jnp.zeros_like(racc)

        @pl.loop(0, 2)
        def _(k):
            for n in range(4):
                cols = pl.ds(pl.multiple_of(k * (C // 2) + n * LAST_W, LAST_W), LAST_W)
                t = E[:, cols] * cs[:, cols]
                racc[...] += tiles(t)
                U[...] += nt(t.astype(BF16), nrm[:, cols]).reshape(DEEP, 2, S, B)

    def col_step(it, k):
        @pl.loop(0, CW // 1024)
        def _(n):
            part = pl.ds(pl.multiple_of(n * 1024, 1024), 1024)
            cols = pl.ds(pl.multiple_of(k * CW + n * 1024, 1024), 1024)
            total = jnp.zeros((8, 1024), F32)
            for r in range(R // 8):
                scale = sscol[r * 8:(r + 1) * 8, :]
                total = total + E[r * 8:(r + 1) * 8, cols] * jnp.concatenate([scale] * 8, axis=1)
            csum[it, k, :, part] = jnp.sum(total, axis=0, keepdims=True)

    def block(a, b):
        blk = at(a, b)
        s = G[blk, :, 0].reshape(R, B).astype(BF16)
        t = G[blk, :, 1].reshape(R, B).astype(BF16)
        rows = pl.ds(pl.multiple_of(blk * R, R), R)
        ET[rows, :] = jnp.exp2(nn(t, nown[...]) * TEACHER).astype(BF16)
        e = jnp.exp2(nn(s, nown[...]) * STUDENT).astype(BF16)
        turned = s.astype(F32).T
        suT[:, rows] = turned.astype(BF16)
        PG[...] += nn((turned * iva[blk]).astype(BF16), e)

    def blocks(pairs):
        for a, b in pairs:
            if (a, b) != (0, 0):
                mate_wait(a, b)
            block(a, b)

    def core_sum_send(v, which, ph):
        send(v.at[:, 1 - c], cr.at[which], ph, mate)

    def core_sum_wait(v, which, ph, zph):
        landed(cr.at[which], ph)
        zs[which] = v[:, c] + cr[which]
        for d in range(1, DEEP):
            send(zs.at[which, lax.rem(z + d, DEEP)], zr.at[which, d - 1], zph, along_z(d))

    def z_sum(which, zph):
        landed(zr.at[which], zph)
        total = zs[which, z]
        for d in range(DEEP - 1):
            total = total + zr[which, d]
        return total

    for it in range(ITERS):
        slot(3 * it)
        if it == 0:
            student_chunks(0, 8)
        elif it == 1:
            core_sum_wait(PU, 0, CP, ZP)
        for k in range(CH):
            y_step(it, k)
        slot(3 * it + 1)
        if it == 0:
            student_chunks(8, 16)
        elif it == 1:
            landed(iva.at[pl.ds(0, DP - 1)], INV)
            blocks(((0, 0),))
        elif it == 2:
            blocks(READY_MID)
            late_slot()
        for k in range(CH):
            row_step(it, k)
        if it == ITERS - 1:
            last_pass()
            core_sum_send(U, 1, CU)
        hsrc[it, :, 0:R] = across(racc[...])
        if it == 0:
            hsrc[it, :, R:2 * R] = across(eacc[...])
        wide = 2 * R if it == 0 else R
        to_head(hsrc.at[it, :, pl.ds(0, wide)], lambda e: hr.at[it, e, :, pl.ds(0, wide)], H0 + it)
        slot(3 * it + 2)
        if it == 0:
            core_sum_send(PU, 0, CP)
        elif it == 1:
            blocks(NEAR)
        elif it == 2:
            core_sum_wait(U, 1, CU, ZU)
            blocks(READY_FAR)
        landed(hr.at[it, :, :, pl.ds(0, wide)], H0 + it)
        row_total = hsrc[it, :, 0:R]
        for d in range(HEAD - 1):
            row_total = row_total + hr[it, d, :, 0:R]
        if it == 0:
            exp_total = hsrc[it, :, R:2 * R]
            for d in range(HEAD - 1):
                exp_total = exp_total + hr[it, d, :, R:2 * R]
            iva[i] = 1.0 / exp_total
        if it < ITERS - 1:
            sscol[...] = down(1.0 / (ROWS * row_total))
            for k in range(CH):
                col_step(it + 1, k)
                x_send(it + 1, k)
        if it == 0:
            to_dp(iva.at[i], iva.at[i], INV)

    ssa[i] = 1.0 / row_total
    to_dp(ssa.at[i], ssa.at[i], SS)
    mate_send(LAST + END)
    blocks(READY_LAST)

    target_sum = z_sum(1, ZU)
    student_sum = z_sum(0, ZP)
    own = lax.broadcasted_iota(jnp.int32, (S, R), 1) == lax.broadcasted_iota(jnp.int32, (S, R), 0) + j * S

    def pick(v):
        return jnp.sum(jnp.where(own, v, 0.0), axis=1, keepdims=True)

    own_rows = pl.ds(pl.multiple_of(j * S, S), S)
    in_half = pl.ds(pl.multiple_of(lax.rem(j, 8) * S, S), S)
    unit_rows = G[i, j // 8, 0, in_half]
    target_mean = target_sum * pick(ssa[i])
    exp_inv = pick(iva[i])
    unit_grad = GRAD * (student_sum * exp_inv - target_mean)
    row_dot = jnp.sum(unit_rows * unit_grad, axis=1, keepdims=True)
    agb[c, z] = invn[own_rows, 0:1] * (unit_grad - unit_rows * row_dot)
    for d in (4, 3, 5, 2, 6, 1, 7):
        send(agb.at[c, z], agb.at[c, z], AGZ, along_z(d))
    raw_mean = jnp.sum(unit_rows * target_mean, axis=1, keepdims=True)
    part_loss = jnp.sum(raw_mean * 10.0 + jnp.log(exp_inv), axis=0, keepdims=True)
    ldr[i] = jnp.broadcast_to(part_loss, (1, 128))
    to_dp(ldr.at[i], ldr.at[i], LD)

    landed(ssa.at[pl.ds(0, DP - 1)], SS)
    for k in range(4):
        rows = slice(k * 4 * R, (k + 1) * 4 * R)
        scale = jnp.concatenate([ssa[k * 4 + n] for n in range(4)], axis=1)
        suT[:, rows] = (suT[:, rows].astype(F32) * scale).astype(BF16)

    @pl.loop(0, 2)
    def _(h):
        half = pl.ds(pl.multiple_of(h * (W // 2), W // 2), W // 2)
        mine_half = pl.ds(pl.multiple_of(i * W + h * (W // 2), W // 2), W // 2)
        grad = jnp.zeros((B, W // 2), F32)
        for k in range(4):
            rows = slice(k * 4 * R, (k + 1) * 4 * R)
            grad = grad + nn(suT[:, rows], ET[rows, half])
        unit_cols = nown[:, half].astype(F32)
        normed_grad = GRAD * (PG[:, half] - cs[:, mine_half] * grad)
        col_dot = jnp.sum(unit_cols * normed_grad, axis=0, keepdims=True)
        a2s[h] = (colinv[:, mine_half] * (normed_grad - unit_cols * col_dot)).reshape(DP, B // DP, W // 2)
        for a, b in DP_OFF:
            to = lax.rem(x + a, SIDE) * SIDE + lax.rem(y + b, SIDE)
            send(a2s.at[h, to], a2r.at[h, i], A2A + h, (to, j))
        a2r[h, i] = a2s[h, i]

    landed(ldr.at[pl.ds(0, DP - 1)], LD)
    total = ldr[0]
    for d in range(1, DP):
        total = total + ldr[d]
    lhr[j] = total
    to_head(lhr.at[j], lambda e: lhr.at[j], LH)
    landed(agb.at[c, pl.ds(0, DEEP - 1)], AGZ)
    send(agb.at[c], agb.at[c], AGC, mate)

    def rows_in(h):
        for k in range(DEEP):
            v = agb[h, k]
            high = v.astype(BF16)
            dhi[k, h] = high
            dlo[k, h] = (v - high.astype(F32)).astype(BF16)

    rows_in(c)
    landed(agb.at[1 - c], AGC)
    rows_in(1 - c)
    outs = []
    for n in range(4):
        rows = slice(n * 256, (n + 1) * 256)
        patch = nn(oh[rows, :], dhi[...].reshape(R, B)) + nn(oh[rows, :], dlo[...].reshape(R, B))
        E[0:256, n * 256:(n + 1) * 256] = patch
        outs.append(pltpu.make_async_copy(E.at[pl.ds(0, 256), pl.ds(n * 256, 256)], patch_out.at[pl.ds(n * 256, 256)], osem.at[n]))
        outs[-1].start()
    landed(lhr.at[pl.ds(0, HEAD - 1)], LH)
    total = lhr[0]
    for d in range(1, HEAD):
        total = total + lhr[d]
    loss_out[...] = total * (-1.0 / ROWS)

    for it in range(ITERS):
        for k in range(CH):
            sent(xr.at[it, k], X0 + it * CH + k)
            sent(yr.at[it, k], Y0 + it * CH + k)
        wide = 2 * R if it == 0 else R
        sent(hr.at[it, :, :, pl.ds(0, wide)], H0 + it)
    sent(iva.at[pl.ds(0, DP - 1)], INV)
    sent(ssa.at[pl.ds(0, DP - 1)], SS)
    sent(cr.at[1], CU)
    sent(cr.at[0], CP)
    sent(zr.at[1], ZU)
    sent(zr.at[0], ZP)
    sent(agb.at[c, pl.ds(0, DEEP - 1)], AGZ)
    sent(agb.at[c], AGC)
    sent(ldr.at[pl.ds(0, DP - 1)], LD)
    sent(lhr.at[pl.ds(0, HEAD - 1)], LH)
    whole, half, near = part(i, 0), part(i, 0, 0), beside(i, 0, 0)

    def gsent(like, sid):
        pltpu.make_async_copy(like, like, gsend.at[sid]).wait()

    for u in (0, 1):
        for s in (0, 1):
            gsent(whole, A1(u, s))
            gsent(half, F1(u, s))
            for m in range(4):
                gsent(whole, A2(u, m, s))
                gsent(half, F2(u, m, s))
    for a in range(SIDE):
        for b in range(SIDE):
            if (a, b) != (0, 0):
                gsent(G.at[i, c], MATE(a, b))
                gsent(near, ZED(a, b, 0))
                gsent(near, ZED(a, b, 1))

    for h in (0, 1):
        landed(a2r.at[h, pl.ds(0, DP - 1)], A2A + h)
        for d in range(DP):
            wide_out[:, d * W + h * W // 2:d * W + (h + 1) * W // 2] = a2r[h, d]
    outs.append(pltpu.make_async_copy(wide_out, proto_out, osem.at[4]))
    outs[-1].start()
    for h in (0, 1):
        sent(a2r.at[h, pl.ds(0, DP - 1)], A2A + h)
    for copy in outs:
        copy.wait()


def finish(patches, protos, patch_out, proto_out, patch_buf, proto_buf, isem, osem):
    parts = []
    for source, buf, target, count in ((patches, patch_buf, patch_out, 4), (protos, proto_buf, proto_out, 2)):
        size = source.shape[0] // count
        for n in range(count):
            rows, at = pl.ds(n * size, size), len(parts)
            parts.append((
                pltpu.make_async_copy(source.at[rows], buf.at[rows], isem.at[at]),
                pltpu.make_async_copy(buf.at[rows], target.at[rows], osem.at[at]),
            ))
    for get, _ in parts:
        get.start()
    for get, put in parts:
        get.wait()
        put.start()
    for _, put in parts:
        put.wait()


def on_device(student_patches, teacher_patches, mask_rows, prototypes):
    vm = pltpu.VMEM
    whole = pl.BlockSpec(memory_space=pltpu.VMEM)
    anywhere = pl.BlockSpec(memory_space=pl.ANY)
    results = (
        jax.ShapeDtypeStruct(student_patches.shape, F32),
        jax.ShapeDtypeStruct((B // DP, C), F32),
    )
    patches, protos, loss = pl.pallas_call(
        kernel,
        out_shape=results + (jax.ShapeDtypeStruct((1, 128), F32),),
        in_specs=[whole] * 3 + [anywhere],
        out_specs=(anywhere, anywhere, whole),
        scratch_shapes=[
            vm((1024, R), BF16),
            vm((R, B), BF16),
            vm((R, B), BF16),
            vm((R, 128), F32),
            vm((B, C), BF16),
            vm((B, W), BF16),
            vm((1, C), F32),
            vm((R, C), F32),
            vm((DP, 2, 2, R // 2, B), F32),
            vm((DP * R, W), BF16),
            vm((B, DP * R), BF16),
            vm((B, W), F32),
            vm((DEEP, 2, S, B), F32),
            vm((DEEP, 2, S, B), F32),
            vm((2, DEEP, S, B), F32),
            vm((2, DEEP, S, B), F32),
            vm((2, DEEP - 1, S, B), F32),
            vm((ITERS, CH, 1, CW), F32),
            vm((ITERS, CH, 1, CW), F32),
            vm((ITERS, CH, SIDE - 1, 1, CW), F32),
            vm((ITERS, CH, SIDE - 1, 1, CW), F32),
            vm((1, C), F32),
            vm((R, 128), F32),
            vm((R, 128), F32),
            vm((R, 128), F32),
            vm((ITERS, 1, 2 * R), F32),
            vm((ITERS, HEAD - 1, 1, 2 * R), F32),
            vm((DP, 1, R), F32),
            vm((DP, 1, R), F32),
            vm((2, DEEP, S, B), F32),
            vm((2, DP, B // DP, W // 2), F32),
            vm((2, DP, B // DP, W // 2), F32),
            vm((B // DP, C), F32),
            vm((DEEP, 2, S, B), BF16),
            vm((DEEP, 2, S, B), BF16),
            vm((DP, 1, 128), F32),
            vm((HEAD, 1, 128), F32),
            pltpu.SemaphoreType.DMA((SMALL,)),
            pltpu.SemaphoreType.DMA((SMALL,)),
            pltpu.SemaphoreType.DMA((GATHER,)),
            pltpu.SemaphoreType.DMA((GATHER,)),
            pltpu.SemaphoreType.DMA((CH,)),
            pltpu.SemaphoreType.DMA((5,)),
        ],
        compiler_params=pltpu.CompilerParams(
            collective_id=0, has_side_effects=True, vmem_limit_bytes=63 * 2**20
        ),
    )(student_patches, teacher_patches, mask_rows.reshape(1, R), prototypes)
    patches, protos = pl.pallas_call(
        finish,
        out_shape=results,
        in_specs=[anywhere] * 2,
        out_specs=(anywhere, anywhere),
        scratch_shapes=[
            vm(student_patches.shape, F32),
            vm((B // DP, C), F32),
            pltpu.SemaphoreType.DMA((6,)),
            pltpu.SemaphoreType.DMA((6,)),
        ],
    )(patches, protos)
    return patches, protos, loss[0, 0]


def solution(mesh):
    return jax.shard_map(
        on_device,
        mesh=mesh,
        in_specs=(P("dp", None), P("dp", None), P("dp"), P(None, "head")),
        out_specs=(P("dp", None), P("dp", "head"), P()),
        check_vma=False,
    )
```

time: 108 us -> 91.1 us (0.84)
  Pallas kernels: 102 us -> 88.5 us
  local copies, waits for them, and re-layouts: 4.13 us -> 0 us
    pallas_call x1 -> x2, Pallas kernels: 102 us -> 88.5 us  [the longest x1 86.3 us: on_device(): pl.pallas_call(kernel, out_shape=results + (jax.ShapeDtypeStruct((1, 128)...]
    unnamed x2 -> x0, local copies, waits for them, and re-layouts: 4.13 us -> none
where the time goes in v2:
time: 91.1 us; the launch traced here: 90.9 us
  Pallas kernels  88.5 us (97%)
  between operations  2.41 us (3%)
    pallas_call x1, Pallas kernels, on_device(): pl.pallas_call(kernel, out_shape=results + (jax.ShapeDtypeStruct((1, 128)...  86.3 us
    pallas_call x1, Pallas kernels, on_device(): pl.pallas_call(finish, out_shape=results, in_specs=[anywhere] * 2, out_sp...  2.19 us

profile of v2, /device:TPU:1, one launch (start us, length us, event | category | flops | bytes accessed | tf_op | source)
XLA Modules:
  0.0 90.9 jit_solution(7977696531668469473)
XLA Ops:
  0.6 86.3 %shard_map.67 = (f32[1024,256]{1,0:T(8,128)}, f32[16,8192]{1,0:T(8,128)}, f32[1,128]{1,0:T(1,128)}) custom-call(bf16[1024,256]{1,0:T(8,128)(2,1)} %student.1, bf16[1024,256]{1,0:T(8,128)(2,1)} %teacher.1, s32[1,512]{1,0:T(1,128)} %bitcast.3, bf16[256,8192]{1,0:T(8,128)(2,1)} %proto.1), custom_call_target="tpu_custom_call" | custom-call | tf_op jit(solution)/shard_map/pallas_call | solution.py:598
  87.0 2.2 %shard_map.68 = (f32[1024,256]{1,0:T(8,128)}, f32[16,8192]{1,0:T(8,128)}) custom-call(f32[1024,256]{1,0:T(8,128)} %get-tuple-element.8.patches, f32[16,8192]{1,0:T(8,128)} %get-tuple-element.9.protos), custom_call_target="tpu_custom_call" | custom-call | tf_op jit(solution)/shard_map/pallas_call | solution.py:652

commit v3 on v2

--- a/solution.py
+++ b/solution.py
@@ -29,6 +29,7 @@
 X0, Y0, H0 = 0, ITERS * CH, 2 * ITERS * CH
 INV, SS, CU, ZU, CP, ZP, AGZ, AGC, LD, LH, A2A = range(H0 + ITERS, H0 + ITERS + 11)
 SMALL = A2A + 2
+XS, YS = X0, Y0
 
 
 def far_first(sides):
@@ -38,11 +39,12 @@
 
 DP_OFF, HEAD_OFF = far_first((SIDE, SIDE)), far_first((DEEP, 2))
 
-A1, F1 = lambda u, s: u * 2 + s, lambda u, s: 4 + u * 2 + s
-A2, F2 = lambda u, m, s: 8 + (u * 4 + m) * 2 + s, lambda u, m, s: 24 + (u * 4 + m) * 2 + s
-MATE = lambda a, b: 40 + a * 4 + b
-ZED = lambda a, b, s: 56 + (a * 4 + b) * 2 + s
-GATHER = 88
+A1, F1 = lambda u: u, lambda u: 2 + u
+A2, F2 = lambda u, m: 4 + u * 4 + m, lambda u, m: 12 + u * 4 + m
+MATE = lambda a, b: 20 + a * 4 + b
+ZED = 36
+GATHER = 41
+WHOLE, HALF, MATES, BESIDES = range(4)
 PLANE, BESIDE = 176, 80
 SHIFT = (0, 3, 1, 2)
 
@@ -55,8 +57,8 @@
     return jnp.dot(a, b, preferred_element_type=F32)
 
 
-def kernel(student, teacher, mask, proto, patch_out, proto_out, loss_out,
-           oh, su, tu, invn, nrm, nown, colinv, E, G, ET, suT, PG,
+def kernel(student_hbm, teacher_hbm, mask_hbm, proto, patch_out, proto_out, loss_out,
+           student, teacher, mask, loss, oh, su, tu, invn, nrm, nown, colinv, E, G, ET, suT, PG,
            U, PU, cr, zs, zr, csum, ysum, xr, yr, cs, racc, eacc, sscol,
            hsrc, hr, iva, ssa, agb, a2s, a2r, wide_out, dhi, dlo, ldr, lhr,
            psend, precv, gsend, grecv, lsem, osem):
@@ -69,16 +71,24 @@
         cols = pl.ds(k * CW, CW)
         return pltpu.make_async_copy(proto.at[:, cols], nrm.at[:, cols], lsem.at[k])
 
+    def patch_copy(k):
+        return pltpu.make_async_copy((teacher_hbm, student_hbm)[k], (teacher, student)[k], lsem.at[CH + k])
+
+    mask_copy = pltpu.make_async_copy(mask_hbm, mask, lsem.at[CH + 2])
+
+    barrier = pltpu.get_barrier_semaphore()
+    mask_copy.start()
+    for k in (0, 1):
+        patch_copy(k).start()
     for k in range(CH):
         proto_copy(k).start()
-
-    barrier = pltpu.get_barrier_semaphore()
     for d in range(1, DP):
         pl.semaphore_signal(barrier, inc=1, device_id=(lax.rem(i + d, DP), j), device_id_type=MESH)
         pl.semaphore_signal(barrier, inc=1, device_id=(i, lax.rem(j + d, HEAD)), device_id_type=MESH)
 
-    def send(src, dst, ph, dev):
-        pltpu.make_async_remote_copy(src, dst, psend.at[ph], precv.at[ph], device_id=dev, device_id_type=MESH).start()
+    def send(src, dst, ph, dev, leave=None):
+        leave = ph if leave is None else leave
+        pltpu.make_async_remote_copy(src, dst, psend.at[leave], precv.at[ph], device_id=dev, device_id_type=MESH).start()
 
     def landed(like, ph):
         pltpu.make_async_copy(like, like, precv.at[ph]).wait()
@@ -121,16 +131,19 @@
         first = which * PLANE + s * (BESIDE // 2)
         return G.at[blk, c, :, pl.ds(pl.multiple_of(first, 8), BESIDE // 2)]
 
-    def z_send(pairs):
+    def gcopy(ref, kind, sid, dev):
+        pltpu.make_async_remote_copy(ref, ref, gsend.at[kind], grecv.at[sid], device_id=dev, device_id_type=MESH).start()
+
+    def gwait(like, sid):
+        pltpu.make_async_copy(like, like, grecv.at[sid]).wait()
+
+    both = G.at[0, c, :, pl.ds(0, PLANE)]
+    both_halves = G.at[0, c, :, pl.ds(0, PLANE // 2)]
+
+    def z_send(pairs, batch):
         for a, b in pairs:
             for s in (0, 1):
-                gcopy(beside(at(a, b), odd, s), ZED(a, b, s), along_z(1 if s == 0 else DEEP - 1)).start()
-
-    def gcopy(ref, sid, dev):
-        return pltpu.make_async_remote_copy(ref, ref, gsend.at[sid], grecv.at[sid], device_id=dev, device_id_type=MESH)
-
-    def gwait(ref, sid):
-        pltpu.make_async_copy(ref, ref, grecv.at[sid]).wait()
+                gcopy(beside(at(a, b), odd, s), BESIDES, ZED + batch, along_z(1 if s == 0 else DEEP - 1))
 
     def n1(s):
         return (at(1 if s == 0 else 3, 0), j)
@@ -140,45 +153,39 @@
 
     def a1_send(u):
         for s in (0, 1):
-            gcopy(part(at(0, 0), u), A1(u, s), n1(s)).start()
+            gcopy(part(at(0, 0), u), WHOLE, A1(u), n1(s))
 
     def a1_wait(u):
-        for s in (0, 1):
-            gwait(part(at(3 if s == 0 else 1, 0), u), A1(u, s))
+        gwait(both, A1(u))
 
     def f1_send(u):
         for s in (0, 1):
-            gcopy(part(at(3 if s == 0 else 1, 0), u, s), F1(u, s), n1(s)).start()
+            gcopy(part(at(3 if s == 0 else 1, 0), u, s), HALF, F1(u), n1(s))
 
     def f1_wait(u):
-        for s in (0, 1):
-            gwait(part(at(2, 0), u, s), F1(u, s))
+        gwait(both_halves, F1(u))
 
     def a2_send(u, m):
         for s in (0, 1):
-            gcopy(part(at(SHIFT[m], 0), u), A2(u, m, s), n2(s)).start()
+            gcopy(part(at(SHIFT[m], 0), u), WHOLE, A2(u, m), n2(s))
 
     def a2_wait(u, m):
-        for s in (0, 1):
-            gwait(part(at(SHIFT[m], 3 if s == 0 else 1), u), A2(u, m, s))
+        gwait(both, A2(u, m))
 
     def f2_send(u, m):
         for s in (0, 1):
-            gcopy(part(at(SHIFT[m], 3 if s == 0 else 1), u, s), F2(u, m, s), n2(s)).start()
+            gcopy(part(at(SHIFT[m], 3 if s == 0 else 1), u, s), HALF, F2(u, m), n2(s))
 
     def f2_wait(u, m):
-        for s in (0, 1):
-            gwait(part(at(SHIFT[m], 2), u, s), F2(u, m, s))
-
-    def mate_send(pairs):
+        gwait(both_halves, F2(u, m))
+
+    def mate_send(pairs, batch):
+        gwait(G.at[pl.ds(0, len(pairs)), c, :, pl.ds(0, BESIDE)], ZED + batch)
         for a, b in pairs:
-            for s in (0, 1):
-                gwait(beside(at(a, b), 1 - odd, s), ZED(a, b, s))
-            gcopy(G.at[at(a, b), c], MATE(a, b), mate).start()
+            gcopy(G.at[at(a, b), c], MATES, MATE(a, b), mate)
 
     def mate_wait(a, b):
-        ref = G.at[at(a, b), 1 - c]
-        pltpu.make_async_copy(ref, ref, grecv.at[MATE(b, a)]).wait()
+        gwait(G.at[0, c], MATE(b, a))
 
     NEAR = ((1, 0), (3, 0), (0, 1), (0, 3))
     MID = ((2, 0), (0, 2), (3, 1), (3, 3))
@@ -187,21 +194,20 @@
     END = ((2, 2),)
     READY_MID = ((2, 0), (0, 2), (3, 3))
     READY_FAR = ((3, 1), (1, 1), (1, 3))
-    READY_LAST = ((2, 3), (3, 2), (1, 2), (2, 1), (2, 2))
+    READY_LAST = ((2, 3), (3, 2), (1, 2), (2, 1))
 
     def slot(n):
         if n in (0, 1):
             a1_send(n)
             a2_send(n, 0)
-        elif n in (2, 3):
-            u = n - 2
-            a1_wait(u)
-            f1_send(u)
-            a2_wait(u, 0)
-            f2_send(u, 0)
-            a2_send(u, 1)
-            if u == 1:
-                z_send(NEAR)
+        elif n == 2:
+            a1_wait(0)
+            f1_send(0)
+            a2_wait(0, 0)
+            f2_send(0, 0)
+            a2_send(0, 1)
+        elif n == 3:
+            a2_send(1, 1)
         elif n == 4:
             a2_wait(0, 1)
             f2_send(0, 1)
@@ -216,29 +222,40 @@
             a2_send(0, 3)
             a2_send(1, 3)
             f2_wait(1, 0)
-            mate_send(NEAR)
-            z_send(MID)
+            z_send(MID, 1)
         elif n == 6:
+            for u in (0, 1):
+                a2_wait(u, 3)
+                f2_send(u, 3)
+                f2_wait(u, 2)
+            z_send(LAST, 3)
+        elif n == 7:
+            mate_send(MID, 1)
+        elif n == 8:
+            mate_send(FAR, 2)
+            f2_wait(0, 3)
+            f2_wait(1, 3)
+            z_send(END, 4)
+
+    def later_slot(n):
+        if n == 2:
+            a1_wait(1)
+            f1_send(1)
+            a2_wait(1, 0)
+            f2_send(1, 0)
+            z_send(NEAR, 0)
+        elif n == 4:
+            mate_send(NEAR, 0)
+        elif n == 5:
             for u in (0, 1):
                 a2_wait(u, 2)
                 f2_send(u, 2)
                 f2_wait(u, 1)
-            z_send(FAR)
-        elif n == 7:
-            for u in (0, 1):
-                a2_wait(u, 3)
-                f2_send(u, 3)
-            mate_send(MID)
+            z_send(FAR, 2)
         elif n == 8:
-            f2_wait(0, 3)
-            f2_wait(1, 3)
-            z_send(END)
-            mate_send(FAR)
-
-    def late_slot():
-        f2_wait(0, 2)
-        f2_wait(1, 2)
-        z_send(LAST)
+            mate_send(LAST, 3)
+
+    mask_copy.wait()
 
     @pl.loop(0, 8)
     def _(k):
@@ -251,11 +268,13 @@
         inverse = lax.rsqrt(jnp.sum(rows * rows, axis=1, keepdims=True) + EPS)
         return (rows * inverse).astype(BF16), inverse
 
+    patch_copy(0).wait()
+    unit_t, _ = unit(teacher)
+    tu[...] = unit_t
+    patch_copy(1).wait()
     unit_s, inv_s = unit(student)
     su[...] = unit_s
     invn[...] = jnp.broadcast_to(inv_s, (R, 128))
-    unit_t, _ = unit(teacher)
-    tu[...] = unit_t
     for half in (0, 1):
         rows = slice(half * (R // 2), (half + 1) * (R // 2))
         G[i, half, 0] = su[rows, :].astype(F32)
@@ -263,7 +282,7 @@
 
     def x_send(it, k):
         for d in (2, 1, 3):
-            send(csum.at[it, k], xr.at[it, k, d - 1], X0 + it * CH + k, along_x(d))
+            send(csum.at[it, k], xr.at[it, k, d - 1], X0 + it * CH + k, along_x(d), XS)
 
     for k in range(CH):
         proto_copy(k).wait()
@@ -318,7 +337,7 @@
         landed(xr.at[it, k], X0 + it * CH + k)
         ysum[it, k] = csum[it, k] + xr[it, k, 0] + xr[it, k, 1] + xr[it, k, 2]
         for d in (2, 1, 3):
-            send(ysum.at[it, k], yr.at[it, k, d - 1], Y0 + it * CH + k, along_y(d))
+            send(ysum.at[it, k], yr.at[it, k, d - 1], Y0 + it * CH + k, along_y(d), YS)
 
     def row_step(it, k):
         landed(yr.at[it, k], Y0 + it * CH + k)
@@ -401,9 +420,9 @@
         elif it == 1:
             landed(iva.at[pl.ds(0, DP - 1)], INV)
             blocks(((0, 0),))
+            later_slot(4)
         elif it == 2:
             blocks(READY_MID)
-            late_slot()
         for k in range(CH):
             row_step(it, k)
         if it == ITERS - 1:
@@ -417,11 +436,14 @@
         slot(3 * it + 2)
         if it == 0:
             core_sum_send(PU, 0, CP)
+            later_slot(2)
         elif it == 1:
             blocks(NEAR)
+            later_slot(5)
         elif it == 2:
             core_sum_wait(U, 1, CU, ZU)
             blocks(READY_FAR)
+            later_slot(8)
         landed(hr.at[it, :, :, pl.ds(0, wide)], H0 + it)
         row_total = hsrc[it, :, 0:R]
         for d in range(HEAD - 1):
@@ -441,8 +463,9 @@
 
     ssa[i] = 1.0 / row_total
     to_dp(ssa.at[i], ssa.at[i], SS)
-    mate_send(LAST + END)
-    blocks(READY_LAST)
+    blocks(READY_LAST[:2])
+    mate_send(END, 4)
+    blocks(READY_LAST[2:] + END)
 
     target_sum = z_sum(1, ZU)
     student_sum = z_sum(0, ZP)
@@ -519,12 +542,13 @@
     total = lhr[0]
     for d in range(1, HEAD):
         total = total + lhr[d]
-    loss_out[...] = total * (-1.0 / ROWS)
-
+    loss[...] = total * (-1.0 / ROWS)
+    outs.append(pltpu.make_async_copy(loss, loss_out, osem.at[5]))
+    outs[-1].start()
+
+    sent(xr, XS)
+    sent(yr, YS)
     for it in range(ITERS):
-        for k in range(CH):
-            sent(xr.at[it, k], X0 + it * CH + k)
-            sent(yr.at[it, k], Y0 + it * CH + k)
         wide = 2 * R if it == 0 else R
         sent(hr.at[it, :, :, pl.ds(0, wide)], H0 + it)
     sent(iva.at[pl.ds(0, DP - 1)], INV)
@@ -537,24 +561,14 @@
     sent(agb.at[c], AGC)
     sent(ldr.at[pl.ds(0, DP - 1)], LD)
     sent(lhr.at[pl.ds(0, HEAD - 1)], LH)
-    whole, half, near = part(i, 0), part(i, 0, 0), beside(i, 0, 0)
-
-    def gsent(like, sid):
-        pltpu.make_async_copy(like, like, gsend.at[sid]).wait()
-
-    for u in (0, 1):
-        for s in (0, 1):
-            gsent(whole, A1(u, s))
-            gsent(half, F1(u, s))
-            for m in range(4):
-                gsent(whole, A2(u, m, s))
-                gsent(half, F2(u, m, s))
-    for a in range(SIDE):
-        for b in range(SIDE):
-            if (a, b) != (0, 0):
-                gsent(G.at[i, c], MATE(a, b))
-                gsent(near, ZED(a, b, 0))
-                gsent(near, ZED(a, b, 1))
+
+    def gsent(like, kind):
+        pltpu.make_async_copy(like, like, gsend.at[kind]).wait()
+
+    gsent(G.at[pl.ds(0, 10), c, :, pl.ds(0, PLANE)], WHOLE)
+    gsent(G.at[pl.ds(0, 10), c, :, pl.ds(0, PLANE // 2)], HALF)
+    gsent(G.at[pl.ds(0, DP - 1), c], MATES)
+    gsent(G.at[pl.ds(0, DP - 1), c, :, pl.ds(0, BESIDE)], BESIDES)
 
     for h in (0, 1):
         landed(a2r.at[h, pl.ds(0, DP - 1)], A2A + h)
@@ -589,7 +603,6 @@
 
 def on_device(student_patches, teacher_patches, mask_rows, prototypes):
     vm = pltpu.VMEM
-    whole = pl.BlockSpec(memory_space=pltpu.VMEM)
     anywhere = pl.BlockSpec(memory_space=pl.ANY)
     results = (
         jax.ShapeDtypeStruct(student_patches.shape, F32),
@@ -598,9 +611,13 @@
     patches, protos, loss = pl.pallas_call(
         kernel,
         out_shape=results + (jax.ShapeDtypeStruct((1, 128), F32),),
-        in_specs=[whole] * 3 + [anywhere],
-        out_specs=(anywhere, anywhere, whole),
+        in_specs=[anywhere] * 4,
+        out_specs=(anywhere,) * 3,
         scratch_shapes=[
+            vm(student_patches.shape, BF16),
+            vm(student_patches.shape, BF16),
+            vm((1, R), jnp.int32),
+            vm((1, 128), F32),
             vm((1024, R), BF16),
             vm((R, B), BF16),
             vm((R, B), BF16),
@@ -640,10 +657,10 @@
             vm((HEAD, 1, 128), F32),
             pltpu.SemaphoreType.DMA((SMALL,)),
             pltpu.SemaphoreType.DMA((SMALL,)),
+            pltpu.SemaphoreType.DMA((4,)),
             pltpu.SemaphoreType.DMA((GATHER,)),
-            pltpu.SemaphoreType.DMA((GATHER,)),
-            pltpu.SemaphoreType.DMA((CH,)),
-            pltpu.SemaphoreType.DMA((5,)),
+            pltpu.SemaphoreType.DMA((CH + 3,)),
+            pltpu.SemaphoreType.DMA((6,)),
         ],
         compiler_params=pltpu.CompilerParams(
             collective_id=0, has_side_effects=True, vmem_limit_bytes=63 * 2**20

time: 91.1 us -> 86.2 us (0.946)
  Pallas kernels: 88.5 us -> 83.7 us
    pallas_call x1, Pallas kernels: 86.3 us -> 81.5 us  [on_device(): pl.pallas_call(kernel, out_shape=results + (jax.ShapeDtypeStruct((1, 128)...]
where the time goes in v3:
time: 86.2 us; the launch traced here: 86.1 us
  Pallas kernels  83.7 us (97%)
  between operations  2.41 us (3%)
    pallas_call x1, Pallas kernels, on_device(): pl.pallas_call(kernel, out_shape=results + (jax.ShapeDtypeStruct((1, 128)...  81.5 us
    pallas_call x1, Pallas kernels, on_device(): pl.pallas_call(finish, out_shape=results, in_specs=[anywhere] * 2, out_sp...  2.19 us

profile of v3, /device:TPU:1, one launch (start us, length us, event | category | flops | bytes accessed | tf_op | source)
XLA Modules:
  0.0 86.1 jit_solution(3484214004805769143)
XLA Ops:
  0.6 81.5 %shard_map.67 = (f32[1024,256]{1,0:T(8,128)}, f32[16,8192]{1,0:T(8,128)}, f32[1,128]{1,0:T(1,128)}) custom-call(bf16[1024,256]{1,0:T(8,128)(2,1)} %student_hbm.1, bf16[1024,256]{1,0:T(8,128)(2,1)} %teacher_hbm.1, s32[1,512]{1,0:T(1,128)} %bitcast.3, bf16[256,8192]{1,0:T(8,128)(2,1)} %proto.1), custom_call_target="tpu_custom_call" | custom-call | tf_op jit(solution)/shard_map/pallas_call | solution.py:611
  82.2 2.2 %shard_map.68 = (f32[1024,256]{1,0:T(8,128)}, f32[16,8192]{1,0:T(8,128)}) custom-call(f32[1024,256]{1,0:T(8,128)} %get-tuple-element.8.patches, f32[16,8192]{1,0:T(8,128)} %get-tuple-element.9.protos), custom_call_target="tpu_custom_call" | custom-call | tf_op jit(solution)/shard_map/pallas_call | solution.py:669

commit v4 on v3

--- a/solution.py
+++ b/solution.py
@@ -43,7 +43,7 @@
 A2, F2 = lambda u, m: 4 + u * 4 + m, lambda u, m: 12 + u * 4 + m
 MATE = lambda a, b: 20 + a * 4 + b
 ZED = 36
-GATHER = 41
+GATHER = 42
 WHOLE, HALF, MATES, BESIDES = range(4)
 PLANE, BESIDE = 176, 80
 SHIFT = (0, 3, 1, 2)
@@ -96,12 +96,6 @@
     def sent(like, ph):
         pltpu.make_async_copy(like, like, psend.at[ph]).wait()
 
-    def along_x(d):
-        return (lax.rem(x + d, SIDE) * SIDE + y, j)
-
-    def along_y(d):
-        return (x * SIDE + lax.rem(y + d, SIDE), j)
-
     def to_dp(src, dst, ph):
         for a, b in DP_OFF:
             send(src, dst, ph, (lax.rem(x + a, SIDE) * SIDE + lax.rem(y + b, SIDE), j))
@@ -119,6 +113,12 @@
     def at(dp_, dq_):
         pp, qq = lax.rem(p + dp_, SIDE), lax.rem(q + dq_, SIDE)
         return (pp * SIDE + qq) * (1 - c) + (qq * SIDE + pp) * c
+
+    def first_axis(d):
+        return (at(0, d), j)
+
+    def second_axis(d):
+        return (at(d, 0), j)
 
     odd = lax.rem(z, 2)
 
@@ -188,54 +188,61 @@
         gwait(G.at[0, c], MATE(b, a))
 
     NEAR = ((1, 0), (3, 0), (0, 1), (0, 3))
-    MID = ((2, 0), (0, 2), (3, 1), (3, 3))
+    MID, MID_B = ((2, 0), (0, 2)), ((3, 1), (3, 3))
     FAR = ((3, 2), (1, 1), (1, 3))
     LAST = ((2, 1), (2, 3), (1, 2))
     END = ((2, 2),)
-    READY_MID = ((2, 0), (0, 2), (3, 3))
+    READY_MID, READY_MID_B = ((2, 0), (0, 2)), ((3, 3),)
     READY_FAR = ((3, 1), (1, 1), (1, 3))
     READY_LAST = ((2, 3), (3, 2), (1, 2), (2, 1))
 
     def slot(n):
-        if n in (0, 1):
-            a1_send(n)
-            a2_send(n, 0)
+        if n == 0:
+            a1_send(0)
+            a2_send(0, 0)
+            a2_send(1, 0)
+        elif n == 1:
+            a1_send(1)
         elif n == 2:
             a1_wait(0)
             f1_send(0)
+            a2_send(0, 1)
             a2_wait(0, 0)
             f2_send(0, 0)
-            a2_send(0, 1)
+            a2_send(0, 2)
         elif n == 3:
             a2_send(1, 1)
-        elif n == 4:
+            a2_send(1, 2)
+            f1_wait(0)
+            a2_send(0, 3)
             a2_wait(0, 1)
             f2_send(0, 1)
-            a2_send(0, 2)
-            a2_send(1, 2)
-            f1_wait(0)
+        elif n == 4:
+            f1_wait(1)
+            a2_send(1, 3)
+            a2_wait(0, 2)
+            f2_send(0, 2)
             f2_wait(0, 0)
-        elif n == 5:
-            a2_wait(1, 1)
-            f2_send(1, 1)
-            f1_wait(1)
-            a2_send(0, 3)
-            a2_send(1, 3)
             f2_wait(1, 0)
             z_send(MID, 1)
+        elif n == 5:
+            for u, m in ((1, 1), (1, 2), (0, 3)):
+                a2_wait(u, m)
+                f2_send(u, m)
+            z_send(MID_B, 2)
         elif n == 6:
-            for u in (0, 1):
-                a2_wait(u, 3)
-                f2_send(u, 3)
-                f2_wait(u, 2)
-            z_send(LAST, 3)
+            a2_wait(1, 3)
+            f2_send(1, 3)
+            f2_wait(0, 2)
+            f2_wait(1, 2)
+            z_send(LAST, 4)
+            mate_send(MID_B, 2)
         elif n == 7:
-            mate_send(MID, 1)
-        elif n == 8:
-            mate_send(FAR, 2)
             f2_wait(0, 3)
             f2_wait(1, 3)
-            z_send(END, 4)
+            z_send(END, 5)
+        elif n == 8:
+            mate_send(LAST, 4)
 
     def later_slot(n):
         if n == 2:
@@ -247,13 +254,14 @@
         elif n == 4:
             mate_send(NEAR, 0)
         elif n == 5:
-            for u in (0, 1):
-                a2_wait(u, 2)
-                f2_send(u, 2)
-                f2_wait(u, 1)
-            z_send(FAR, 2)
+            f2_wait(0, 1)
+            f2_wait(1, 1)
+            z_send(FAR, 3)
+            mate_send(MID, 1)
+        elif n == 7:
+            mate_send(FAR, 3)
         elif n == 8:
-            mate_send(LAST, 3)
+            mate_send(END, 5)
 
     mask_copy.wait()
 
@@ -282,7 +290,7 @@
 
     def x_send(it, k):
         for d in (2, 1, 3):
-            send(csum.at[it, k], xr.at[it, k, d - 1], X0 + it * CH + k, along_x(d), XS)
+            send(csum.at[it, k], xr.at[it, k, d - 1], X0 + it * CH + k, first_axis(d), XS)
 
     for k in range(CH):
         proto_copy(k).wait()
@@ -337,7 +345,7 @@
         landed(xr.at[it, k], X0 + it * CH + k)
         ysum[it, k] = csum[it, k] + xr[it, k, 0] + xr[it, k, 1] + xr[it, k, 2]
         for d in (2, 1, 3):
-            send(ysum.at[it, k], yr.at[it, k, d - 1], Y0 + it * CH + k, along_y(d), YS)
+            send(ysum.at[it, k], yr.at[it, k, d - 1], Y0 + it * CH + k, second_axis(d), YS)
 
     def row_step(it, k):
         landed(yr.at[it, k], Y0 + it * CH + k)
@@ -412,6 +420,8 @@
             student_chunks(0, 8)
         elif it == 1:
             core_sum_wait(PU, 0, CP, ZP)
+        elif it == 2:
+            blocks(READY_MID)
         for k in range(CH):
             y_step(it, k)
         slot(3 * it + 1)
@@ -422,7 +432,8 @@
             blocks(((0, 0),))
             later_slot(4)
         elif it == 2:
-            blocks(READY_MID)
+            blocks(READY_MID_B)
+            later_slot(7)
         for k in range(CH):
             row_step(it, k)
         if it == ITERS - 1:
@@ -463,9 +474,7 @@
 
     ssa[i] = 1.0 / row_total
     to_dp(ssa.at[i], ssa.at[i], SS)
-    blocks(READY_LAST[:2])
-    mate_send(END, 4)
-    blocks(READY_LAST[2:] + END)
+    blocks(READY_LAST + END)
 
     target_sum = z_sum(1, ZU)
     student_sum = z_sum(0, ZP)

time: 86.2 us -> 84.7 us (0.983)
  Pallas kernels: 83.7 us -> 82.1 us
    pallas_call x1, Pallas kernels: 81.5 us -> 79.9 us  [on_device(): pl.pallas_call(kernel, out_shape=results + (jax.ShapeDtypeStruct((1, 128)...]
where the time goes in v4:
time: 84.7 us; the launch traced here: 84.5 us
  Pallas kernels  82.1 us (97%)
  between operations  2.41 us (3%)
    pallas_call x1, Pallas kernels, on_device(): pl.pallas_call(kernel, out_shape=results + (jax.ShapeDtypeStruct((1, 128)...  79.9 us
    pallas_call x1, Pallas kernels, on_device(): pl.pallas_call(finish, out_shape=results, in_specs=[anywhere] * 2, out_sp...  2.19 us

profile of v4, /device:TPU:1, one launch (start us, length us, event | category | flops | bytes accessed | tf_op | source)
XLA Modules:
  0.0 84.5 jit_solution(5063752554154209129)
XLA Ops:
  0.6 79.9 %shard_map.67 = (f32[1024,256]{1,0:T(8,128)}, f32[16,8192]{1,0:T(8,128)}, f32[1,128]{1,0:T(1,128)}) custom-call(bf16[1024,256]{1,0:T(8,128)(2,1)} %student_hbm.1, bf16[1024,256]{1,0:T(8,128)(2,1)} %teacher_hbm.1, s32[1,512]{1,0:T(1,128)} %bitcast.3, bf16[256,8192]{1,0:T(8,128)(2,1)} %proto.1), custom_call_target="tpu_custom_call" | custom-call | tf_op jit(solution)/shard_map/pallas_call | solution.py:620
  80.6 2.2 %shard_map.68 = (f32[1024,256]{1,0:T(8,128)}, f32[16,8192]{1,0:T(8,128)}) custom-call(f32[1024,256]{1,0:T(8,128)} %get-tuple-element.8.patches, f32[16,8192]{1,0:T(8,128)} %get-tuple-element.9.protos), custom_call_target="tpu_custom_call" | custom-call | tf_op jit(solution)/shard_map/pallas_call | solution.py:678

commit v5 on v4

--- a/solution.py
+++ b/solution.py
@@ -241,8 +241,6 @@
             f2_wait(0, 3)
             f2_wait(1, 3)
             z_send(END, 5)
-        elif n == 8:
-            mate_send(LAST, 4)
 
     def later_slot(n):
         if n == 2:
@@ -261,6 +259,8 @@
         elif n == 7:
             mate_send(FAR, 3)
         elif n == 8:
+            mate_send(LAST, 4)
+        elif n == 9:
             mate_send(END, 5)
 
     mask_copy.wait()
@@ -474,6 +474,7 @@
 
     ssa[i] = 1.0 / row_total
     to_dp(ssa.at[i], ssa.at[i], SS)
+    later_slot(9)
     blocks(READY_LAST + END)
 
     target_sum = z_sum(1, ZU)

time: 84.7 us -> 84.7 us (level)
  no operation moved by 1% of the time
where the time goes in v5:
time: 84.7 us; the launch traced here: 84.6 us
  Pallas kernels  82.2 us (97%)
  between operations  2.41 us (3%)
    pallas_call x1, Pallas kernels, on_device(): pl.pallas_call(kernel, out_shape=results + (jax.ShapeDtypeStruct((1, 128)...  80 us
    pallas_call x1, Pallas kernels, on_device(): pl.pallas_call(finish, out_shape=results, in_specs=[anywhere] * 2, out_sp...  2.19 us

profile of v5, /device:TPU:1, one launch (start us, length us, event | category | flops | bytes accessed | tf_op | source)
XLA Modules:
  0.0 84.6 jit_solution(616956221068964742)
XLA Ops:
  0.6 80.0 %shard_map.67 = (f32[1024,256]{1,0:T(8,128)}, f32[16,8192]{1,0:T(8,128)}, f32[1,128]{1,0:T(1,128)}) custom-call(bf16[1024,256]{1,0:T(8,128)(2,1)} %student_hbm.1, bf16[1024,256]{1,0:T(8,128)(2,1)} %teacher_hbm.1, s32[1,512]{1,0:T(1,128)} %bitcast.3, bf16[256,8192]{1,0:T(8,128)(2,1)} %proto.1), custom_call_target="tpu_custom_call" | custom-call | tf_op jit(solution)/shard_map/pallas_call | solution.py:621
  80.6 2.2 %shard_map.68 = (f32[1024,256]{1,0:T(8,128)}, f32[16,8192]{1,0:T(8,128)}) custom-call(f32[1024,256]{1,0:T(8,128)} %get-tuple-element.8.patches, f32[16,8192]{1,0:T(8,128)} %get-tuple-element.9.protos), custom_call_target="tpu_custom_call" | custom-call | tf_op jit(solution)/shard_map/pallas_call | solution.py:679
